TPU v7x, 768 devices: a whole 4x8x12 slice. The times are simulated.
768 devices in a mesh: space: 192 (over z, y_hi, x, core), event: 4 (over y_lo).
Axes of the slice: x: 4, y: 8 (y_hi: 2, y_lo: 4; y = y_hi * 4 + y_lo), z: 12, core: 2. Of those that a mesh axis runs over, the one named last changes fastest.
Arguments:
- green: bfloat16 [8, 512, 2, 6, 24576], P(None, 'event', None, None, 'space'), may hold values from -6 to 6
- strain: bfloat16 [96, 8, 2, 6, 24576], P('event', None, None, None, 'space'), may hold values from -6 to 6
- perturb: float32 [24576], P('space'), may hold values from -6 to 6
- pairs: int32 [96, 512], P(None, 'event'), may hold values 0 or 1
Outputs:
- hessian: float32 [24576], P(('space', 'event'))
All inputs are finite; a program needn't handle non-finite values. No bound on the sum of `pairs` on one device may be relied on, other than what follows from the above.
Results may differ from a plain program's by a relative error of at most 0.00096.
Values may be sent and summed in bfloat16 or wider, within the bound.
No kernel may reach another device: no remote copies, remote signals or barrier semaphores. Data moves between devices by JAX's collectives and lax.ppermute only.
A program may use at most 32 MiB of HBM per device.

v0:
```python
import math

import jax
import jax.numpy as jnp
from jax import lax
from jax.sharding import PartitionSpec as P


def body(green, strain, perturb, pairs):
    freqs = green.shape[0]
    recv_dev = green.shape[1]
    comps = green.shape[3]
    cells = green.shape[4]
    n_space = lax.axis_size("space")
    n_event = lax.axis_size("event")
    everything = lax.all_gather(strain, "event", axis=0, tiled=True)
    events = everything.shape[0]
    scale_one = 1.0 / math.sqrt(12.0 * cells * n_space)
    scale_two = 1.0 / math.sqrt(12.0 * events * freqs * recv_dev * n_event)
    weighted = (everything.astype(jnp.float32) * perturb).astype(jnp.bfloat16)
    w_real = weighted[:, :, 0].reshape(events, freqs, -1)
    w_imag = weighted[:, :, 1].reshape(events, freqs, -1)
    combo = jnp.stack([jnp.stack([w_real, -w_imag], 2), jnp.stack([w_imag, w_real], 2)], 1)
    flat_green = green.reshape(freqs, recv_dev, 2, -1)
    partial_data = jnp.einsum(
        "frpk,eqfpk->fqer", flat_green, combo, preferred_element_type=jnp.float32
    )
    mask = pairs.astype(jnp.float32)
    total = lax.psum(partial_data, "space")
    resid = (scale_one * total * mask).astype(jnp.bfloat16)
    back_in = jnp.stack(
        [jnp.stack([resid[:, 0], resid[:, 1]], 2), jnp.stack([resid[:, 1], -resid[:, 0]], 2)], 1
    )
    back = jnp.einsum("fqepr,frpk->fqek", back_in, flat_green, preferred_element_type=jnp.float32)
    flat_strain = everything.reshape(events, freqs, 2, -1).astype(jnp.float32)
    terms = jnp.einsum("fqek,efqk->k", back, flat_strain)
    local_cells = terms.reshape(comps, cells).sum(0)
    summed = lax.psum_scatter(local_cells, "event", scatter_dimension=0, tiled=True)
    return scale_two * summed


def solution(mesh):
    in_specs = (
        P(None, "event", None, None, "space"),
        P("event", None, None, None, "space"),
        P("space"),
        P(None, "event"),
    )
    out_specs = P(("space", "event"))
    return jax.shard_map(body, mesh=mesh, in_specs=in_specs, out_specs=out_specs, check_vma=False)
```

profile of v0, /device:TPU:1, one launch (start us, length us, event | category | flops | bytes accessed | tf_op | source)
XLA Modules:
  0.0 2306.5 jit_solution(14114825249975394145)
XLA Ops:
  6.5 0.0 all-gather.2.cloned.1.call-start
  6.5 1.9 copy.37
  8.5 0.0 all-gather.2.cloned.1.call-update
  8.5 0.0 copy-start.2
  8.5 0.0 all-reduce.3.cloned.1.call-start
  8.6 7.1 copy.42
  15.7 61.2 %all-gather.2.cloned.1.call-done = bf16[96,8,2,6,128]{4,1,3,2,0:T(8,128)(2,1)} async-done(((bf16[24,8,2,6,128]{4,1,3,2,0:T(8,128)(2,1)}), bf16[96,8,2,6,128]{4,1,3,2,0:T(8,128)(2,1)}) %all-gather.2.cloned.1.call-update) | async-done | bytes 2359312 | tf_op jit(solution)/shard_map/all_gather | solution.py:16
  76.9 0.0 copy-done.2
  76.9 2.1 multiply_convert_fusion
  79.0 0.2 slice_bitcast_fusion
  79.2 0.2 copy_negate_fusion
  79.5 0.2 copy.39
  79.7 0.4 maximum_bitcast_fusion
  80.1 0.0 copy-start.1
  80.1 2.3 fusion.4
  82.3 0.0 all-reduce.3.cloned.1.call-update
  82.4 1.3 dynamic-slice
  84.3 0.0 copy-done.1
  84.3 2202.1 %all-reduce.3.cloned.1.call-done = f32[8,2,96,128]{3,2,1,0:T(8,128)} async-done(((f32[8,2,96,128]{3,2,1,0:T(8,128)}), f32[8,2,96,128]{3,2,1,0:T(8,128)}) %all-reduce.3.cloned.1.call-update) | async-done | bytes 786448 | tf_op jit(solution)/shard_map/psum | solution.py:29
  2286.5 1.2 multiply_convert_fusion.1
  2287.7 0.1 maximum_bitcast_fusion.2
  2287.8 0.0 copy-start
  2287.8 1.2 convolution_bitcast_fusion
  2289.0 0.5 copy-done
  2289.5 2.6 multiply_reduce_fusion
  2292.1 7.0 all-reduce
  2299.1 0.6 dynamic-slice_multiply_fusion
  (4 shorter events, 0.1 us)
Async XLA Ops:
  6.5 70.4 %all-gather.2.cloned.1.call-start = ((), (), s32[]{:S(2)}) async-start(), calls=%async_computation | async-start | bytes 2949120 | tf_op jit(solution)/shard_map/all_gather | solution.py:16
  8.5 68.4 %copy-start.2 = (f32[128]{0:T(128)S(1)}, f32[128]{0:T(128)}, u32[]{:S(2)}) copy-start(f32[128]{0:T(128)} %param.6) | copy-start | bytes 1540
  8.5 2277.9 %all-reduce.3.cloned.1.call-start = ((), (), s32[]{:S(2)}) async-start(), calls=%async_computation.1 | async-start | bytes 1572864 | tf_op jit(solution)/shard_map/psum | solution.py:29
  80.1 4.2 copy-start.1
  2287.8 1.7 copy-start
Sparse Core Ops, SparseCore 0:
  9.7 67.1 all-gather.1
  82.5 2203.9 all-reduce.2
where the time goes:
time: 2310 us
  waiting for transfers between devices  2260 us (98%)
    psum x1, waiting for transfers between devices, body(): total = lax.psum(partial_data, 'space')  2200 us
    all_gather x1, waiting for transfers between devices, body(): everything = lax.all_gather(strain, 'event', axis=0, tiled=True)  61.2 us
  transfers between devices with their start and end apart: 2, of which 2 were waited for; matrix products, arithmetic and copies ran while one was open for 0% of the time, Pallas kernels for 0%

commit v1 on v0

v1 whole, which is shorter than its diff:
```python
import math

import jax
import jax.numpy as jnp
from jax import lax
from jax.experimental import pallas as pl
from jax.experimental.pallas import tpu as pltpu
from jax.sharding import Mesh, PartitionSpec as P

PIECES = 2
SPACE = ("z_far", "z_near", "y_hi", "x", "core")
NEAR = ("z_near", "x", "core")
FAR = ("z_far", "y_hi")
WHOLE = pl.BlockSpec(memory_space=pltpu.VMEM)


def exchange(parts, axes):
    return lax.all_to_all(parts, axes, 0, 0, tiled=True)


def spread(block, axes):
    n = lax.axis_size(axes)
    return exchange(jnp.broadcast_to(block[None], (n,) + block.shape), axes)


def wide(ref, *at):
    return jnp.concatenate([ref[at + (c,)] for c in range(ref.shape[len(at)])], 1)


def forward_kernel(own, n_event, *refs):
    pieces, (perturb_ref, green_ref, out_ref, all_ref) = refs[:-4], refs[-4:]
    per_piece = 2 * n_event - 1
    recv = out_ref.shape[-1]
    comps, cells = all_ref.shape[1], all_ref.shape[3]
    perturb = perturb_ref[...]

    for base in range(0, len(pieces), per_piece):
        piece = pieces[base:base + per_piece]
        freqs = piece[0].shape[0]
        start = base // per_piece * freqs

        def step(i, carry):
            f = start + i
            blocks = [wide(piece[0], i).astype(jnp.float32)]
            for low, high in zip(piece[1::2], piece[2::2]):
                blocks.append(wide(low, i).astype(jnp.float32) + wide(high, i).astype(jnp.float32))
            strain = jnp.concatenate(blocks, 0)
            for c in range(comps):
                all_ref[f, c] = strain[:, c * cells:(c + 1) * cells].astype(all_ref.dtype)
            weighted = (strain * perturb).astype(jnp.bfloat16)
            both = lax.dot_general(
                weighted, wide(green_ref, f), (((1,), (1,)), ((), ())), preferred_element_type=jnp.float32
            )
            rows = []
            for k in range(n_event):
                real = both[2 * own * k:2 * own * k + own]
                imag = both[2 * own * k + own:2 * own * (k + 1)]
                rows += [real[:, :recv] - imag[:, recv:], imag[:, :recv] + real[:, recv:]]
            out_ref[f] = jnp.concatenate(rows, 0).astype(out_ref.dtype)
            return carry

        lax.fori_loop(0, freqs, step, 0, unroll=2)


def backward_kernel(own, n_event, all_ref, resid_ref, green_ref, out_ref):
    freqs, comps, n_rows, cells = all_ref.shape

    def step(f, acc):
        resid = resid_ref[f].astype(jnp.float32)
        sides = []
        for k in range(n_event):
            real = resid[2 * own * k:2 * own * k + own]
            imag = resid[2 * own * k + own:2 * own * (k + 1)]
            sides += [jnp.concatenate([real, imag], 1), jnp.concatenate([imag, -real], 1)]
        sides = jnp.concatenate(sides, 0).astype(jnp.bfloat16)
        back = jnp.dot(sides, wide(green_ref, f), preferred_element_type=jnp.float32)
        for c in range(comps):
            terms = back[:, c * cells:(c + 1) * cells] * all_ref[f, c].astype(jnp.float32)
            for j in range(0, n_rows, 8):
                acc = acc + terms[j:j + 8]
        return acc

    acc = lax.fori_loop(0, freqs, step, jnp.zeros((8, cells), jnp.float32), unroll=2)
    acc = acc.sum(0, keepdims=True)
    parts, width = out_ref.shape
    for j in range(parts):
        out_ref[j:j + 1] = acc[:, j * width:(j + 1) * width]


def hop(blocks, k):
    n = lax.axis_size("event")
    ups = [lax.ppermute(up, "event", [(i, i + 1) for i in range(k - 1, n - 1)]) for up, _ in blocks]
    downs = [lax.ppermute(down, "event", [(i, i - 1) for i in range(1, n + 1 - k)]) for _, down in blocks]
    return list(zip(ups, downs))


def body(green, strain, perturb, pairs):
    freqs, recv, _, comps, cells = green.shape
    own = strain.shape[0]
    n_event = lax.axis_size("event")
    near = lax.axis_size(NEAR)
    far = lax.axis_size(FAR)
    me = lax.axis_index("event")
    events = own * n_event
    k_all = comps * cells
    n_rows = 2 * events
    tall = freqs * n_rows // near
    scale_one = 1.0 / math.sqrt(12.0 * cells * near * far)
    scale_two = 1.0 / math.sqrt(12.0 * events * freqs * recv * n_event)

    mine = strain.transpose(1, 3, 2, 0, 4).reshape(freqs, comps, 2 * own, cells)
    flat_green = green.transpose(0, 3, 2, 1, 4).reshape(freqs, comps, 2 * recv, cells)
    share = freqs // PIECES
    pieces = [mine[h * share:(h + 1) * share] for h in range(PIECES)]
    hops = [hop([(p, p) for p in pieces], 1)]
    first, flat_green = lax.optimization_barrier((hops[0][0], flat_green))
    hops[0][0] = first
    for k in range(2, n_event):
        hops.append(hop(hops[-1], k))
    blocks = []
    for h in range(PIECES):
        blocks.append(pieces[h])
        for k in range(1, n_event):
            blocks += [hops[k - 1][h][0], hops[n_event - k - 1][h][1]]
    wide_perturb = jnp.tile(perturb, comps)[None]

    order = jnp.stack(
        [lax.dynamic_slice_in_dim(pairs, ((me - k) % n_event) * own, own, 0) for k in range(n_event)], 0
    )
    mask = jnp.broadcast_to(order.astype(jnp.float32)[:, None], (n_event, 2, own, recv))
    offset = (lax.axis_index(NEAR) * tall) % n_rows
    mask = lax.dynamic_slice_in_dim(mask.reshape(n_rows, recv), offset, tall, 0)

    macs = freqs * n_rows * k_all * 2 * recv
    params = dict(
        compiler_params=pltpu.CompilerParams(vmem_limit_bytes=16 * 2**20),
        cost_estimate=pl.CostEstimate(flops=2 * macs, bytes_accessed=6_000_000, transcendentals=0),
    )
    partial, all_strain = pl.pallas_call(
        lambda *refs: forward_kernel(own, n_event, *refs),
        in_specs=[WHOLE] * (len(blocks) + 2),
        out_specs=[WHOLE] * 2,
        out_shape=[
            jax.ShapeDtypeStruct((freqs, n_rows, recv), jnp.bfloat16),
            jax.ShapeDtypeStruct((freqs, comps, n_rows, cells), jnp.bfloat16),
        ],
        name="forward",
        **params,
    )(*blocks, wide_perturb, flat_green)
    partial, mask = lax.optimization_barrier((partial, mask))

    got = exchange(partial.reshape(near, tall, recv), NEAR)
    summed = got.astype(jnp.float32).sum(0).astype(jnp.bfloat16)
    total = spread(summed, FAR).astype(jnp.float32).sum(0)
    resid = (scale_one * total * mask).astype(jnp.bfloat16)
    resid = spread(resid, NEAR).reshape(freqs, n_rows, recv)

    local_cells = pl.pallas_call(
        lambda *refs: backward_kernel(own, n_event, *refs),
        in_specs=[WHOLE] * 3,
        out_specs=WHOLE,
        out_shape=jax.ShapeDtypeStruct((n_event, cells // n_event), jnp.float32),
        name="backward",
        **params,
    )(all_strain, resid, flat_green)
    got = exchange(local_cells, "event")
    return scale_two * got.sum(0)


def solution(mesh):
    n_event = mesh.shape["event"]
    fine = Mesh(mesh.devices.reshape(6, 2, 2, 4, 2, n_event), SPACE + ("event",))
    in_specs = (
        P(None, "event", None, None, SPACE),
        P("event", None, None, None, SPACE),
        P(SPACE),
        P(None, "event"),
    )
    out_specs = P(SPACE + ("event",))
    return jax.shard_map(body, mesh=fine, in_specs=in_specs, out_specs=out_specs, check_vma=False)
```

time: 2310 us -> 134 us (0.06)
  waiting for transfers between devices: 2260 us -> 17.6 us
  blocking collectives: 7.01 us -> 77.1 us
    psum x1 -> x0, waiting for transfers between devices: 2200 us -> none  [body(): total = lax.psum(partial_data, 'space')]
    all_to_all x0 -> x4, blocking collectives: none -> 77.1 us  [exchange(): return lax.all_to_all(parts, axes, 0, 0, tiled=True)]
    all_gather x1 -> x0, waiting for transfers between devices: 61.2 us -> none  [body(): everything = lax.all_gather(strain, 'event', axis=0, tiled=True)]
  transfers between devices with their start and end apart: 2 -> 12, of which waited for: 2 -> 4; matrix products, arithmetic and copies ran while one was open for 0% -> 3% of each run, Pallas kernels for 0% -> 0%
where the time goes in v1:
time: 134 us; the launch traced here: 133 us
  blocking collectives  77.1 us (58%)
  starting transfers between devices  21.9 us (16%)
  waiting for transfers between devices  17.6 us (13%)
  local copies, waits for them, and re-layouts  8.42 us (6%)
  Pallas kernels  5.42 us (4%)
  other arithmetic  2.06 us (2%)
    all_to_all x4, blocking collectives, exchange(): return lax.all_to_all(parts, axes, 0, 0, tiled=True)  77.1 us
    ppermute x6, waiting for transfers between devices, hop(): lax.ppermute(down, 'event', [(i, i - 1) for i in range(1, n + 1 - k)])  17.6 us
    ppermute x6, starting transfers between devices, hop(): lax.ppermute(up, 'event', [(i, i + 1) for i in range(k - 1, n - 1)])  14.2 us
    ppermute x6, starting transfers between devices, hop(): lax.ppermute(down, 'event', [(i, i - 1) for i in range(1, n + 1 - k)])  7.71 us
    pallas_call x1, Pallas kernels, body(): pl.pallas_call(lambda *refs: forward_kernel(own, n_event, *refs), in_spec...  3.33 us
    transpose x1, local copies, waits for them, and re-layouts, body(): green.transpose(0, 3, 2, 1, 4).reshape(freqs, comps, 2 * recv, cells)  2.75 us
  transfers between devices with their start and end apart: 12, of which 4 were waited for; matrix products, arithmetic and copies ran while one was open for 3% of the time, Pallas kernels for 0%

profile of v1, /device:TPU:1, one launch (start us, length us, event | category | flops | bytes accessed | tf_op | source)
XLA Modules:
  0.0 132.8 jit_solution(10150835398208988277)
XLA Ops:
  0.0 0.0 copy-start
  0.0 1.5 %fusion = (bf16[4,6,2,24,128]{4,2,1,0,3:T(2,128)(2,1)S(1)}, bf16[4,6,2,24,128]{4,2,1,0,3:T(2,128)(2,1)S(1)}) fusion(bf16[8,6,2,24,128]{4,2,1,0,3:T(2,128)(2,1)} %bitcast.38), kind=kLoop, calls=%fused_computation.11 | loop fusion | bytes 1179648 | tf_op jit(solution)/shard_map/slice | solution.py:114
  1.5 0.1 copy.12
  1.6 4.8 %collective-permute-start = (bf16[4,6,48,128]{3,2,1,0:T(8,128)(2,1)S(1)}, bf16[4,6,48,128]{3,2,1,0:T(8,128)(2,1)}, u32[]{:S(2)}, u32[]{:S(2)}) collective-permute-start(bf16[4,6,48,128]{3,2,1,0:T(8,128)(2,1)S(1)} %bitcast.28), channel_id=1, source_target_pairs={{0,1},{1,2},{2,3},{4,5},{5,6},{6,7},{8,9},{9,10},{10,11},{12,13},{... | collective-permute-start | bytes 884744 | tf_op jit(solution)/shard_map/ppermute | solution.py:92
  6.3 1.3 collective-permute-start.1
  7.6 0.1 copy.14
  7.7 0.0 copy-start.3
  7.7 1.3 collective-permute-start.7
  9.0 5.3 %collective-permute-start.6 = (bf16[4,6,48,128]{3,2,1,0:T(8,128)(2,1)S(1)}, bf16[4,6,48,128]{3,2,1,0:T(8,128)(2,1)}, u32[]{:S(2)}, u32[]{:S(2)}) collective-permute-start(bf16[4,6,48,128]{3,2,1,0:T(8,128)(2,1)S(1)} %bitcast.32), channel_id=1, source_target_pairs={{0,1},{1,2},{2,3},{4,5},{5,6},{6,7},{8,9},{9,10},{10,11},{12,13},{... | collective-permute-start | bytes 884744 | tf_op jit(solution)/shard_map/ppermute | solution.py:92
  14.4 2.8 %copy.13 = bf16[8,6,2,128,128]{4,3,2,1,0:T(8,128)(2,1)S(1)} copy(bf16[8,6,2,128,128]{4,2,1,3,0:T(2,128)(2,1)} %bitcast.37) | data formatting | bytes 6291456 | tf_op jit(solution)/shard_map/transpose | solution.py:112
  17.1 0.0 copy-done.3
  17.1 0.0 collective-permute-done.refs_1_
  17.1 0.0 collective-permute-done.1.refs_6_
  17.2 1.3 collective-permute-start.2
  18.5 1.4 %collective-permute-start.4 = (bf16[4,6,48,128]{3,2,1,0:T(8,128)(2,1)}, bf16[4,6,48,128]{3,2,1,0:T(8,128)(2,1)}, u32[]{:S(2)}, u32[]{:S(2)}) collective-permute-start(bf16[4,6,48,128]{3,2,1,0:T(8,128)(2,1)} %collective-permute-done.refs_1_), channel_id=1, source_target_pairs={{1,2},{2,3},{5,6},{6,7},{9,10},{10,11},{13,14},{14,15},{17,18},{18... | collective-permute-start | bytes 884744 | tf_op jit(solution)/shard_map/ppermute | solution.py:92
  19.8 0.0 collective-permute-done.7.refs_13_
  19.8 1.3 collective-permute-start.8
  21.1 0.0 collective-permute-done.6.refs_8_
  21.1 1.4 %collective-permute-start.10 = (bf16[4,6,48,128]{3,2,1,0:T(8,128)(2,1)}, bf16[4,6,48,128]{3,2,1,0:T(8,128)(2,1)}, u32[]{:S(2)}, u32[]{:S(2)}) collective-permute-start(bf16[4,6,48,128]{3,2,1,0:T(8,128)(2,1)} %collective-permute-done.6.refs_8_), channel_id=1, source_target_pairs={{1,2},{2,3},{5,6},{6,7},{9,10},{10,11},{13,14},{14,15},{17,18},{18... | collective-permute-start | bytes 884744 | tf_op jit(solution)/shard_map/ppermute | solution.py:92
  22.5 0.0 copy-done
  22.5 5.9 %collective-permute-done.2.refs_4_ = bf16[4,6,48,128]{3,2,1,0:T(8,128)(2,1)} collective-permute-done((bf16[4,6,48,128]{3,2,1,0:T(8,128)(2,1)}, bf16[4,6,48,128]{3,2,1,0:T(8,128)(2,1)}, u32[]{:S(2)}, u32[]{:S(2)}) %collective-permute-start.2) | collective-permute-done | bytes 294944 | tf_op jit(solution)/shard_map/ppermute | solution.py:93
  28.5 1.3 collective-permute-start.3
  29.7 0.0 collective-permute-done.4.refs_3_
  29.8 0.7 collective-permute-start.5
  30.4 2.4 %collective-permute-done.8.refs_11_ = bf16[4,6,48,128]{3,2,1,0:T(8,128)(2,1)} collective-permute-done((bf16[4,6,48,128]{3,2,1,0:T(8,128)(2,1)}, bf16[4,6,48,128]{3,2,1,0:T(8,128)(2,1)}, u32[]{:S(2)}, u32[]{:S(2)}) %collective-permute-start.8) | collective-permute-done | bytes 294944 | tf_op jit(solution)/shard_map/ppermute | solution.py:93
  32.9 1.3 collective-permute-start.9
  34.2 0.0 collective-permute-done.10.refs_10_
  34.2 0.7 collective-permute-start.11
  34.9 0.0 copy-done.5
  34.9 0.6 constant_dynamic-slice_fusion
  35.5 3.4 %collective-permute-done.3.refs_2_ = bf16[4,6,48,128]{3,2,1,0:T(8,128)(2,1)S(1)} collective-permute-done((bf16[4,6,48,128]{3,2,1,0:T(8,128)(2,1)}, bf16[4,6,48,128]{3,2,1,0:T(8,128)(2,1)S(1)}, u32[]{:S(2)}, u32[]{:S(2)}) %collective-permute-start.3) | collective-permute-done | bytes 294944 | tf_op jit(solution)/shard_map/ppermute | solution.py:93
  39.0 0.0 collective-permute-done.5.refs_5_
  39.0 5.8 %collective-permute-done.9.refs_9_ = bf16[4,6,48,128]{3,2,1,0:T(8,128)(2,1)S(1)} collective-permute-done((bf16[4,6,48,128]{3,2,1,0:T(8,128)(2,1)}, bf16[4,6,48,128]{3,2,1,0:T(8,128)(2,1)S(1)}, u32[]{:S(2)}, u32[]{:S(2)}) %collective-permute-start.9) | collective-permute-done | bytes 294944 | tf_op jit(solution)/shard_map/ppermute | solution.py:93
  44.8 0.0 collective-permute-done.11.refs_12_
  44.8 1.0 copy-done.4
  45.8 3.3 %forward.1 = (bf16[8,192,128]{2,1,0:T(8,128)(2,1)S(1)}, bf16[8,6,192,128]{3,2,1,0:T(8,128)(2,1)S(1)}) custom-call(bf16[4,6,48,128]{3,2,1,0:T(8,128)(2,1)S(1)} %bitcast.30, bf16[4,6,48,128]{3,2,1,0:T(8,128)(2,1)} %collective-permute-done.refs_1_, bf16[4,6,48,128]{3,2,1,0:T(8,128)(2,1)S(1)} %collective-permute-done.3.refs_2_, ...), custom_call_target="tpu_custom_call" | custom-call | flops 603979776 | bytes 6000000 | tf_op jit(solution)/shard_map/forward/pallas_call | solution.py:139
  49.1 0.0 copy-start.1
  49.1 1.4 %copy-done.1 = bf16[8,6,192,128]{3,2,1,0:T(8,128)(2,1)} copy-done((bf16[8,6,192,128]{3,2,1,0:T(8,128)(2,1)}, bf16[8,6,192,128]{3,2,1,0:T(8,128)(2,1)S(1)}, u32[]{:S(2)}) %copy-start.1) | copy-done | bytes 2359320
  50.5 19.1 %all_to_all.24 = bf16[16,96,128]{2,1,0:T(8,128)(2,1)S(1)} all-to-all(bf16[16,96,128]{2,1,0:T(8,128)(2,1)S(1)} %bitcast.34), channel_id=1, replica_groups=mesh['z_far'=6,'z_near'=2,'y_hi'=2,'x'=4,'core'=2,'event'=4] {'z_near','..., dimensions={0} | all-to-all | bytes 786432 | tf_op jit(solution)/shard_map/all_to_all | solution.py:18
  69.6 0.7 reduce_sum.30
  70.3 0.9 broadcast_in_dim.7
  71.2 35.2 %all_to_all.25 = bf16[12,96,128]{2,1,0:T(8,128)(2,1)S(1)} all-to-all(bf16[12,96,128]{2,1,0:T(8,128)(2,1)S(1)} %broadcast_in_dim.7), channel_id=1, replica_groups=mesh['z_far'=6,'z_near'=2,'y_hi'=2,'x'=4,'core'=2,'event'=4] {'z_far','y..., dimensions={0} | all-to-all | bytes 589824 | tf_op jit(solution)/shard_map/all_to_all | solution.py:18
  106.5 0.8 multiply_convert_fusion
  107.3 0.1 broadcast_in_dim.8
  107.3 14.3 %all_to_all.26 = bf16[16,96,128]{2,1,0:T(8,128)(2,1)S(1)} all-to-all(bf16[16,96,128]{2,1,0:T(8,128)(2,1)S(1)} %broadcast_in_dim.8), channel_id=1, replica_groups=mesh['z_far'=6,'z_near'=2,'y_hi'=2,'x'=4,'core'=2,'event'=4] {'z_near','..., dimensions={0} | all-to-all | bytes 786432 | tf_op jit(solution)/shard_map/all_to_all | solution.py:18
  121.6 2.1 %backward.1 = f32[4,32]{1,0:T(4,128)S(1)} custom-call(bf16[8,6,192,128]{3,2,1,0:T(8,128)(2,1)S(1)} %copy-done.2, bf16[8,192,128]{2,1,0:T(8,128)(2,1)S(1)} %bitcast.27, bf16[8,6,256,128]{3,2,1,0:T(8,128)(2,1)S(1)} %bitcast.26), custom_call_target="tpu_custom_call" | custom-call | flops 603979776 | bytes 6000000 | tf_op jit(solution)/shard_map/backward/pallas_call | solution.py:158
  123.7 8.5 %all_to_all.27 = f32[4,1,32]{2,1,0:T(1,128)S(1)} all-to-all(f32[4,1,32]{2,1,0:T(1,128)S(1)} %bitcast.36), channel_id=1, replica_groups=mesh['z_far'=6,'z_near'=2,'y_hi'=2,'x'=4,'core'=2,'event'=4] {'event'}, dimensions={0} | all-to-all | bytes 1024 | tf_op jit(solution)/shard_map/all_to_all | solution.py:18
  132.3 0.5 broadcast_multiply_fusion
  (11 shorter events, 0.1 us)
Async XLA Ops:
  0.0 22.5 %copy-start = (f32[128]{0:T(128)S(1)}, f32[128]{0:T(128)}, u32[]{:S(2)}) copy-start(f32[128]{0:T(128)} %param.6) | copy-start | bytes 1540
  1.6 15.6 %collective-permute-start = (bf16[4,6,48,128]{3,2,1,0:T(8,128)(2,1)S(1)}, bf16[4,6,48,128]{3,2,1,0:T(8,128)(2,1)}, u32[]{:S(2)}, u32[]{:S(2)}) collective-permute-start(bf16[4,6,48,128]{3,2,1,0:T(8,128)(2,1)S(1)} %bitcast.28), channel_id=1, source_target_pairs={{0,1},{1,2},{2,3},{4,5},{5,6},{6,7},{8,9},{9,10},{10,11},{12,13},{... | collective-permute-start | bytes 884744 | tf_op jit(solution)/shard_map/ppermute | solution.py:92
  6.3 10.8 %collective-permute-start.1 = (bf16[4,6,48,128]{3,2,1,0:T(8,128)(2,1)S(1)}, bf16[4,6,48,128]{3,2,1,0:T(8,128)(2,1)}, u32[]{:S(2)}, u32[]{:S(2)}) collective-permute-start(bf16[4,6,48,128]{3,2,1,0:T(8,128)(2,1)S(1)} %bitcast.29), channel_id=1, source_target_pairs={{1,0},{2,1},{3,2},{5,4},{6,5},{7,6},{9,8},{10,9},{11,10},{13,12},{... | collective-permute-start | bytes 884744 | tf_op jit(solution)/shard_map/ppermute | solution.py:93
  7.7 9.4 %copy-start.3 = (bf16[4,6,2,24,128]{4,3,2,1,0:T(8,128)(2,1)}, bf16[4,6,2,24,128]{4,3,2,1,0:T(8,128)(2,1)S(1)}, u32[]{:S(2)}) copy-start(bf16[4,6,2,24,128]{4,3,2,1,0:T(8,128)(2,1)S(1)} %copy.14) | copy-start | bytes 884740
  7.7 12.1 %collective-permute-start.7 = (bf16[4,6,48,128]{3,2,1,0:T(8,128)(2,1)S(1)}, bf16[4,6,48,128]{3,2,1,0:T(8,128)(2,1)}, u32[]{:S(2)}, u32[]{:S(2)}) collective-permute-start(bf16[4,6,48,128]{3,2,1,0:T(8,128)(2,1)S(1)} %bitcast.31), channel_id=1, source_target_pairs={{1,0},{2,1},{3,2},{5,4},{6,5},{7,6},{9,8},{10,9},{11,10},{13,12},{... | collective-permute-start | bytes 884744 | tf_op jit(solution)/shard_map/ppermute | solution.py:93
  9.0 12.1 %collective-permute-start.6 = (bf16[4,6,48,128]{3,2,1,0:T(8,128)(2,1)S(1)}, bf16[4,6,48,128]{3,2,1,0:T(8,128)(2,1)}, u32[]{:S(2)}, u32[]{:S(2)}) collective-permute-start(bf16[4,6,48,128]{3,2,1,0:T(8,128)(2,1)S(1)} %bitcast.32), channel_id=1, source_target_pairs={{0,1},{1,2},{2,3},{4,5},{5,6},{6,7},{8,9},{9,10},{10,11},{12,13},{... | collective-permute-start | bytes 884744 | tf_op jit(solution)/shard_map/ppermute | solution.py:92
  14.4 20.5 %copy-start.5 = (s32[96,128]{1,0:T(8,128)S(1)}, s32[96,128]{1,0:T(8,128)}, u32[]{:S(2)}) copy-start(s32[96,128]{1,0:T(8,128)} %param.7) | copy-start | bytes 147460
  17.2 11.3 %collective-permute-start.2 = (bf16[4,6,48,128]{3,2,1,0:T(8,128)(2,1)}, bf16[4,6,48,128]{3,2,1,0:T(8,128)(2,1)}, u32[]{:S(2)}, u32[]{:S(2)}) collective-permute-start(bf16[4,6,48,128]{3,2,1,0:T(8,128)(2,1)} %collective-permute-done.1.refs_6_), channel_id=1, source_target_pairs={{1,0},{2,1},{5,4},{6,5},{9,8},{10,9},{13,12},{14,13},{17,16},{18,1... | collective-permute-start | bytes 884744 | tf_op jit(solution)/shard_map/ppermute | solution.py:93
  18.5 11.3 %collective-permute-start.4 = (bf16[4,6,48,128]{3,2,1,0:T(8,128)(2,1)}, bf16[4,6,48,128]{3,2,1,0:T(8,128)(2,1)}, u32[]{:S(2)}, u32[]{:S(2)}) collective-permute-start(bf16[4,6,48,128]{3,2,1,0:T(8,128)(2,1)} %collective-permute-done.refs_1_), channel_id=1, source_target_pairs={{1,2},{2,3},{5,6},{6,7},{9,10},{10,11},{13,14},{14,15},{17,18},{18... | collective-permute-start | bytes 884744 | tf_op jit(solution)/shard_map/ppermute | solution.py:92
  19.8 13.0 %collective-permute-start.8 = (bf16[4,6,48,128]{3,2,1,0:T(8,128)(2,1)}, bf16[4,6,48,128]{3,2,1,0:T(8,128)(2,1)}, u32[]{:S(2)}, u32[]{:S(2)}) collective-permute-start(bf16[4,6,48,128]{3,2,1,0:T(8,128)(2,1)} %collective-permute-done.7.refs_13_), channel_id=1, source_target_pairs={{1,0},{2,1},{5,4},{6,5},{9,8},{10,9},{13,12},{14,13},{17,16},{18,1... | collective-permute-start | bytes 884744 | tf_op jit(solution)/shard_map/ppermute | solution.py:93
  21.1 13.0 %collective-permute-start.10 = (bf16[4,6,48,128]{3,2,1,0:T(8,128)(2,1)}, bf16[4,6,48,128]{3,2,1,0:T(8,128)(2,1)}, u32[]{:S(2)}, u32[]{:S(2)}) collective-permute-start(bf16[4,6,48,128]{3,2,1,0:T(8,128)(2,1)} %collective-permute-done.6.refs_8_), channel_id=1, source_target_pairs={{1,2},{2,3},{5,6},{6,7},{9,10},{10,11},{13,14},{14,15},{17,18},{18... | collective-permute-start | bytes 884744 | tf_op jit(solution)/shard_map/ppermute | solution.py:92
  28.5 10.5 %collective-permute-start.3 = (bf16[4,6,48,128]{3,2,1,0:T(8,128)(2,1)}, bf16[4,6,48,128]{3,2,1,0:T(8,128)(2,1)S(1)}, u32[]{:S(2)}, u32[]{:S(2)}) collective-permute-start(bf16[4,6,48,128]{3,2,1,0:T(8,128)(2,1)} %collective-permute-done.2.refs_4_), channel_id=1, source_target_pairs={{1,0},{5,4},{9,8},{13,12},{17,16},{21,20},{25,24},{29,28},{33,32},... | collective-permute-start | bytes 884744 | tf_op jit(solution)/shard_map/ppermute | solution.py:93
  29.8 9.2 %collective-permute-start.5 = (bf16[4,6,48,128]{3,2,1,0:T(8,128)(2,1)}, bf16[4,6,48,128]{3,2,1,0:T(8,128)(2,1)S(1)}, u32[]{:S(2)}, u32[]{:S(2)}) collective-permute-start(bf16[4,6,48,128]{3,2,1,0:T(8,128)(2,1)} %collective-permute-done.4.refs_3_), channel_id=1, source_target_pairs={{2,3},{6,7},{10,11},{14,15},{18,19},{22,23},{26,27},{30,31},{34,35... | collective-permute-start | bytes 884744 | tf_op jit(solution)/shard_map/ppermute | solution.py:92
  32.9 11.9 %collective-permute-start.9 = (bf16[4,6,48,128]{3,2,1,0:T(8,128)(2,1)}, bf16[4,6,48,128]{3,2,1,0:T(8,128)(2,1)S(1)}, u32[]{:S(2)}, u32[]{:S(2)}) collective-permute-start(bf16[4,6,48,128]{3,2,1,0:T(8,128)(2,1)} %collective-permute-done.8.refs_11_), channel_id=1, source_target_pairs={{1,0},{5,4},{9,8},{13,12},{17,16},{21,20},{25,24},{29,28},{33,32},... | collective-permute-start | bytes 884744 | tf_op jit(solution)/shard_map/ppermute | solution.py:93
  34.2 10.6 %collective-permute-start.11 = (bf16[4,6,48,128]{3,2,1,0:T(8,128)(2,1)}, bf16[4,6,48,128]{3,2,1,0:T(8,128)(2,1)S(1)}, u32[]{:S(2)}, u32[]{:S(2)}) collective-permute-start(bf16[4,6,48,128]{3,2,1,0:T(8,128)(2,1)} %collective-permute-done.10.refs_10_), channel_id=1, source_target_pairs={{2,3},{6,7},{10,11},{14,15},{18,19},{22,23},{26,27},{30,31},{34,35... | collective-permute-start | bytes 884744 | tf_op jit(solution)/shard_map/ppermute | solution.py:92
  44.8 1.0 copy-start.4
  49.1 1.4 %copy-start.1 = (bf16[8,6,192,128]{3,2,1,0:T(8,128)(2,1)}, bf16[8,6,192,128]{3,2,1,0:T(8,128)(2,1)S(1)}, u32[]{:S(2)}) copy-start(bf16[8,6,192,128]{3,2,1,0:T(8,128)(2,1)S(1)} %get-tuple-element.15.refs_0_) | copy-start | bytes 7077892
  70.3 51.3 %copy-start.2 = (bf16[8,6,192,128]{3,2,1,0:T(8,128)(2,1)S(1)}, bf16[8,6,192,128]{3,2,1,0:T(8,128)(2,1)}, u32[]{:S(2)}) copy-start(bf16[8,6,192,128]{3,2,1,0:T(8,128)(2,1)} %copy-done.1) | copy-start | bytes 7077892

commit v2 on v0

v2 whole, which is shorter than its diff:
```python
import functools
import math

import jax
import jax.numpy as jnp
from jax import lax
from jax.experimental import pallas as pl
from jax.experimental.pallas import tpu as pltpu
from jax.sharding import Mesh, PartitionSpec as P

PIECES = 2
SPACE = ("z_far", "z_near", "y_hi", "x", "core")
NEAR = ("z_near", "x", "core")
FAR = ("z_far", "y_hi")
WHOLE = pl.BlockSpec(memory_space=pltpu.VMEM)


def exchange(parts, axes):
    return lax.all_to_all(parts, axes, 0, 0, tiled=True)


def wide(ref, *at):
    return jnp.concatenate([ref[at + (c,)] for c in range(ref.shape[len(at)])], 1)


def call(kernel, name, macs, outs, *args):
    single = not isinstance(outs, list)
    return pl.pallas_call(
        kernel,
        in_specs=[WHOLE] * len(args),
        out_specs=WHOLE if single else [WHOLE] * len(outs),
        out_shape=outs,
        name=name,
        compiler_params=pltpu.CompilerParams(vmem_limit_bytes=16 * 2**20),
        cost_estimate=pl.CostEstimate(flops=2 * macs, bytes_accessed=2_000_000, transcendentals=0),
    )(*args)


def forward_kernel(own, n_event, start, *refs):
    done, piece = refs[:1 if start else 0], refs[1 if start else 0:-4]
    perturb_ref, green_ref, out_ref, all_ref = refs[-4:]
    if done:
        out_ref[:start] = done[0][...]
    recv = out_ref.shape[-1]
    freqs, comps, _, cells = all_ref.shape
    perturb = perturb_ref[...]

    def step(i, carry):
        blocks = [wide(piece[0], i).astype(jnp.float32)]
        for low, high in zip(piece[1::2], piece[2::2]):
            blocks.append(wide(low, i).astype(jnp.float32) + wide(high, i).astype(jnp.float32))
        strain = jnp.concatenate(blocks, 0)
        for c in range(comps):
            all_ref[i, c] = strain[:, c * cells:(c + 1) * cells].astype(all_ref.dtype)
        weighted = (strain * perturb).astype(jnp.bfloat16)
        both = lax.dot_general(
            weighted, wide(green_ref, start + i), (((1,), (1,)), ((), ())), preferred_element_type=jnp.float32
        )
        rows = []
        for k in range(n_event):
            real = both[2 * own * k:2 * own * k + own]
            imag = both[2 * own * k + own:2 * own * (k + 1)]
            rows += [real[:, :recv] - imag[:, recv:], imag[:, :recv] + real[:, recv:]]
        out_ref[start + i] = jnp.concatenate(rows, 0).astype(out_ref.dtype)
        return carry

    lax.fori_loop(0, freqs, step, 0, unroll=2)


def near_sum_kernel(parts_ref, out_ref):
    total = parts_ref[0].astype(jnp.float32)
    for i in range(1, parts_ref.shape[0]):
        total = total + parts_ref[i].astype(jnp.float32)
    total = total.astype(out_ref.dtype)
    for i in range(out_ref.shape[0]):
        out_ref[i] = total


def resid_kernel(scale, own, parts_ref, pairs_ref, out_ref):
    total = parts_ref[0].astype(jnp.float32)
    for i in range(1, parts_ref.shape[0]):
        total = total + parts_ref[i].astype(jnp.float32)
    mask = pairs_ref[...].astype(jnp.float32)
    mask = [mask[j:j + own] for j in range(0, mask.shape[0], own)]
    mask = jnp.concatenate([m for m in mask for _ in range(2)], 0)
    resid = (scale * total * mask).astype(out_ref.dtype)
    for i in range(out_ref.shape[0]):
        out_ref[i] = resid


def backward_kernel(own, n_event, *refs):
    pieces, (resid_ref, green_ref, out_ref) = refs[:-3], refs[-3:]
    freqs, comps, n_rows, cells = pieces[0].shape
    acc = jnp.zeros((8, cells), jnp.float32)

    for h, all_ref in enumerate(pieces):

        def step(i, acc):
            resid = resid_ref[h * freqs + i].astype(jnp.float32)
            sides = []
            for k in range(n_event):
                real = resid[2 * own * k:2 * own * k + own]
                imag = resid[2 * own * k + own:2 * own * (k + 1)]
                sides += [jnp.concatenate([real, imag], 1), jnp.concatenate([imag, -real], 1)]
            sides = jnp.concatenate(sides, 0).astype(jnp.bfloat16)
            back = jnp.dot(sides, wide(green_ref, h * freqs + i), preferred_element_type=jnp.float32)
            for c in range(comps):
                terms = back[:, c * cells:(c + 1) * cells] * all_ref[i, c].astype(jnp.float32)
                for j in range(0, n_rows, 8):
                    acc = acc + terms[j:j + 8]
            return acc

        acc = lax.fori_loop(0, freqs, step, acc, unroll=2)
    acc = acc.sum(0, keepdims=True)
    parts, width = out_ref.shape
    for j in range(parts):
        out_ref[j:j + 1] = acc[:, j * width:(j + 1) * width]


def hop(blocks, k):
    n = lax.axis_size("event")
    ups = [lax.ppermute(up, "event", [(i, i + 1) for i in range(k - 1, n - 1)]) for up, _ in blocks]
    downs = [lax.ppermute(down, "event", [(i, i - 1) for i in range(1, n + 1 - k)]) for _, down in blocks]
    return list(zip(ups, downs))


def body(green, strain, perturb, pairs):
    freqs, recv, _, comps, cells = green.shape
    own = strain.shape[0]
    n_event = lax.axis_size("event")
    near = lax.axis_size(NEAR)
    far = lax.axis_size(FAR)
    me = lax.axis_index("event")
    events = own * n_event
    n_rows = 2 * events
    share = freqs // PIECES
    tall = freqs * n_rows // near
    scale_one = 1.0 / math.sqrt(12.0 * cells * near * far)
    scale_two = 1.0 / math.sqrt(12.0 * events * freqs * recv * n_event)
    bf16 = functools.partial(jax.ShapeDtypeStruct, dtype=jnp.bfloat16)

    mine = strain.transpose(1, 3, 2, 0, 4).reshape(freqs, comps, 2 * own, cells)
    pieces = [mine[h * share:(h + 1) * share] for h in range(PIECES)]
    hops = [hop([(p, p) for p in pieces], 1)]
    for k in range(2, n_event):
        if k == n_event - 1:
            last, green = lax.optimization_barrier((hops[-1][-1], green))
            hops[-1][-1] = last
        hops.append(hop(hops[-1], k))
    flat_green = green.transpose(0, 3, 2, 1, 4).reshape(freqs, comps, 2 * recv, cells)

    wide_perturb = jnp.tile(perturb, comps)[None]
    count = tall // (2 * own)
    block = lax.axis_index(NEAR) * count % n_event
    recorded = jnp.concatenate(
        [lax.dynamic_slice_in_dim(pairs, (me - block - j) % n_event * own, own, 0) for j in range(count)], 0
    )

    macs = share * n_rows * comps * cells * 2 * recv
    done, all_strain = [], []
    for h in range(PIECES):
        blocks = [pieces[h]]
        for k in range(1, n_event):
            blocks += [hops[k - 1][h][0], hops[n_event - k - 1][h][1]]
        if h == PIECES - 1:
            blocks, done, recorded = lax.optimization_barrier((blocks, done, recorded))
        partial, part = call(
            functools.partial(forward_kernel, own, n_event, h * share),
            "forward",
            macs,
            [bf16(((h + 1) * share, n_rows, recv)), bf16((share, comps, n_rows, cells))],
            *done, *blocks, wide_perturb, flat_green,
        )
        done = [partial]
        all_strain.append(part)

    got = exchange(partial.reshape(near, tall, recv), NEAR)
    summed = exchange(call(near_sum_kernel, "near_sum", 0, bf16((far, tall, recv)), got), FAR)
    resid = call(
        functools.partial(resid_kernel, scale_one, own), "resid", 0, bf16((near, tall, recv)), summed, recorded
    )
    resid = exchange(resid, NEAR).reshape(freqs, n_rows, recv)
    local_cells = call(
        functools.partial(backward_kernel, own, n_event),
        "backward",
        PIECES * macs,
        jax.ShapeDtypeStruct((n_event, cells // n_event), jnp.float32),
        *all_strain, resid, flat_green,
    )
    return scale_two * exchange(local_cells, "event").sum(0)


def solution(mesh):
    n_event = mesh.shape["event"]
    fine = Mesh(mesh.devices.reshape(6, 2, 2, 4, 2, n_event), SPACE + ("event",))
    in_specs = (
        P(None, "event", None, None, SPACE),
        P("event", None, None, None, SPACE),
        P(SPACE),
        P(None, "event"),
    )
    out_specs = P(SPACE + ("event",))
    return jax.shard_map(body, mesh=fine, in_specs=in_specs, out_specs=out_specs, check_vma=False)
```

time: 2310 us -> 126 us (0.05)
  waiting for transfers between devices: 2260 us -> 21 us
  blocking collectives: 7.01 us -> 73.4 us
    psum x1 -> x0, waiting for transfers between devices: 2200 us -> none  [body(): total = lax.psum(partial_data, 'space')]
    all_to_all x0 -> x4, blocking collectives: none -> 73.4 us  [exchange(): return lax.all_to_all(parts, axes, 0, 0, tiled=True)]
    all_gather x1 -> x0, waiting for transfers between devices: 61.2 us -> none  [body(): everything = lax.all_gather(strain, 'event', axis=0, tiled=True)]
  transfers between devices with their start and end apart: 2 -> 12, of which waited for: 2 -> 5; matrix products, arithmetic and copies ran while one was open for 0% -> 3% of each run, Pallas kernels for 0% -> 2%
where the time goes in v2:
time: 126 us; the launch traced here: 125 us
  blocking collectives  73.4 us (58%)
  waiting for transfers between devices  21 us (17%)
  starting transfers between devices  19.8 us (16%)
  local copies, waits for them, and re-layouts  5.13 us (4%)
  Pallas kernels  4.95 us (4%)
    all_to_all x4, blocking collectives, exchange(): return lax.all_to_all(parts, axes, 0, 0, tiled=True)  73.4 us
    ppermute x6, waiting for transfers between devices, hop(): lax.ppermute(down, 'event', [(i, i - 1) for i in range(1, n + 1 - k)])  19.4 us
    ppermute x6, starting transfers between devices, hop(): lax.ppermute(up, 'event', [(i, i + 1) for i in range(k - 1, n - 1)])  12.1 us
    ppermute x6, starting transfers between devices, hop(): lax.ppermute(down, 'event', [(i, i - 1) for i in range(1, n + 1 - k)])  7.72 us
    pallas_call x5, Pallas kernels, call(): pl.pallas_call(kernel, in_specs=[WHOLE] * len(args), out_specs=WHOLE if s...  4.95 us
    transpose x1, local copies, waits for them, and re-layouts, body(): green.transpose(0, 3, 2, 1, 4).reshape(freqs, comps, 2 * recv, cells)  2.76 us
  transfers between devices with their start and end apart: 12, of which 5 were waited for; matrix products, arithmetic and copies ran while one was open for 3% of the time, Pallas kernels for 2%

profile of v2, /device:TPU:1, one launch (start us, length us, event | category | flops | bytes accessed | tf_op | source)
XLA Modules:
  0.0 125.1 jit_solution(14005320511720889615)
XLA Ops:
  0.0 0.0 copy-start
  0.0 1.5 %fusion = (bf16[4,6,2,24,128]{4,2,1,0,3:T(2,128)(2,1)S(1)}, bf16[4,6,2,24,128]{4,2,1,0,3:T(2,128)(2,1)S(1)}) fusion(bf16[8,6,2,24,128]{4,2,1,0,3:T(2,128)(2,1)} %bitcast.31), kind=kLoop, calls=%fused_computation.6 | loop fusion | bytes 1179648 | tf_op jit(solution)/shard_map/slice | solution.py:143
  1.5 0.1 copy.9
  1.6 4.0 %collective-permute-start.6 = (bf16[4,6,48,128]{3,2,1,0:T(8,128)(2,1)S(1)}, bf16[4,6,48,128]{3,2,1,0:T(8,128)(2,1)S(1)}, u32[]{:S(2)}, u32[]{:S(2)}) collective-permute-start(bf16[4,6,48,128]{3,2,1,0:T(8,128)(2,1)S(1)} %bitcast.20), channel_id=1, source_target_pairs={{0,1},{1,2},{2,3},{4,5},{5,6},{6,7},{8,9},{9,10},{10,11},{12,13},{... | collective-permute-start | bytes 884744 | tf_op jit(solution)/shard_map/ppermute | solution.py:122
  5.6 1.3 %collective-permute-start.8 = (bf16[4,6,48,128]{3,2,1,0:T(8,128)(2,1)S(1)}, bf16[4,6,48,128]{3,2,1,0:T(8,128)(2,1)S(1)}, u32[]{:S(2)}, u32[]{:S(2)}) collective-permute-start(bf16[4,6,48,128]{3,2,1,0:T(8,128)(2,1)S(1)} %bitcast.21), channel_id=1, source_target_pairs={{1,0},{2,1},{3,2},{5,4},{6,5},{7,6},{9,8},{10,9},{11,10},{13,12},{... | collective-permute-start | bytes 884744 | tf_op jit(solution)/shard_map/ppermute | solution.py:123
  6.9 0.1 copy.8
  7.0 1.3 %collective-permute-start.1 = (bf16[4,6,48,128]{3,2,1,0:T(8,128)(2,1)S(1)}, bf16[4,6,48,128]{3,2,1,0:T(8,128)(2,1)S(1)}, u32[]{:S(2)}, u32[]{:S(2)}) collective-permute-start(bf16[4,6,48,128]{3,2,1,0:T(8,128)(2,1)S(1)} %bitcast.23), channel_id=1, source_target_pairs={{1,0},{2,1},{3,2},{5,4},{6,5},{7,6},{9,8},{10,9},{11,10},{13,12},{... | collective-permute-start | bytes 884744 | tf_op jit(solution)/shard_map/ppermute | solution.py:123
  8.3 4.6 %collective-permute-start = (bf16[4,6,48,128]{3,2,1,0:T(8,128)(2,1)S(1)}, bf16[4,6,48,128]{3,2,1,0:T(8,128)(2,1)S(1)}, u32[]{:S(2)}, u32[]{:S(2)}) collective-permute-start(bf16[4,6,48,128]{3,2,1,0:T(8,128)(2,1)S(1)} %bitcast.24), channel_id=1, source_target_pairs={{0,1},{1,2},{2,3},{4,5},{5,6},{6,7},{8,9},{9,10},{10,11},{12,13},{... | collective-permute-start | bytes 884744 | tf_op jit(solution)/shard_map/ppermute | solution.py:122
  12.9 0.0 collective-permute-done.6.refs_2_
  13.0 0.7 collective-permute-start.7
  13.6 0.0 collective-permute-done.8.refs_7_
  13.7 1.3 %collective-permute-start.9 = (bf16[4,6,48,128]{3,2,1,0:T(8,128)(2,1)S(1)}, bf16[4,6,48,128]{3,2,1,0:T(8,128)(2,1)S(1)}, u32[]{:S(2)}, u32[]{:S(2)}) collective-permute-start(bf16[4,6,48,128]{3,2,1,0:T(8,128)(2,1)S(1)} %collective-permute-done.8.refs_7_), channel_id=1, source_target_pairs={{1,0},{2,1},{5,4},{6,5},{9,8},{10,9},{13,12},{14,13},{17,16},{18,1... | collective-permute-start | bytes 884744 | tf_op jit(solution)/shard_map/ppermute | solution.py:123
  15.0 1.3 %collective-permute-done.1.refs_6_ = bf16[4,6,48,128]{3,2,1,0:T(8,128)(2,1)S(1)} collective-permute-done((bf16[4,6,48,128]{3,2,1,0:T(8,128)(2,1)S(1)}, bf16[4,6,48,128]{3,2,1,0:T(8,128)(2,1)S(1)}, u32[]{:S(2)}, u32[]{:S(2)}) %collective-permute-start.1) | collective-permute-done | bytes 294944 | tf_op jit(solution)/shard_map/ppermute | solution.py:123
  16.2 1.3 %collective-permute-start.2 = (bf16[4,6,48,128]{3,2,1,0:T(8,128)(2,1)S(1)}, bf16[4,6,48,128]{3,2,1,0:T(8,128)(2,1)S(1)}, u32[]{:S(2)}, u32[]{:S(2)}) collective-permute-start(bf16[4,6,48,128]{3,2,1,0:T(8,128)(2,1)S(1)} %collective-permute-done.1.refs_6_), channel_id=1, source_target_pairs={{1,0},{2,1},{5,4},{6,5},{9,8},{10,9},{13,12},{14,13},{17,16},{18,1... | collective-permute-start | bytes 884744 | tf_op jit(solution)/shard_map/ppermute | solution.py:123
  17.5 1.6 %collective-permute-done.refs_1_ = bf16[4,6,48,128]{3,2,1,0:T(8,128)(2,1)S(1)} collective-permute-done((bf16[4,6,48,128]{3,2,1,0:T(8,128)(2,1)S(1)}, bf16[4,6,48,128]{3,2,1,0:T(8,128)(2,1)S(1)}, u32[]{:S(2)}, u32[]{:S(2)}) %collective-permute-start) | collective-permute-done | bytes 294944 | tf_op jit(solution)/shard_map/ppermute | solution.py:122
  19.2 0.7 collective-permute-start.4
  19.8 0.0 collective-permute-done.7.refs_4_
  19.9 7.3 %collective-permute-done.9.refs_5_ = bf16[4,6,48,128]{3,2,1,0:T(8,128)(2,1)S(1)} collective-permute-done((bf16[4,6,48,128]{3,2,1,0:T(8,128)(2,1)S(1)}, bf16[4,6,48,128]{3,2,1,0:T(8,128)(2,1)S(1)}, u32[]{:S(2)}, u32[]{:S(2)}) %collective-permute-start.9) | collective-permute-done | bytes 294944 | tf_op jit(solution)/shard_map/ppermute | solution.py:123
  27.2 1.3 %collective-permute-start.10 = (bf16[4,6,48,128]{3,2,1,0:T(8,128)(2,1)S(1)}, bf16[4,6,48,128]{3,2,1,0:T(8,128)(2,1)S(1)}, u32[]{:S(2)}, u32[]{:S(2)}) collective-permute-start(bf16[4,6,48,128]{3,2,1,0:T(8,128)(2,1)S(1)} %collective-permute-done.9.refs_5_), channel_id=1, source_target_pairs={{1,0},{5,4},{9,8},{13,12},{17,16},{21,20},{25,24},{29,28},{33,32},... | collective-permute-start | bytes 884744 | tf_op jit(solution)/shard_map/ppermute | solution.py:123
  28.5 0.7 collective-permute-start.11
  29.1 4.3 %collective-permute-done.2.refs_4_ = bf16[4,6,48,128]{3,2,1,0:T(8,128)(2,1)S(1)} collective-permute-done((bf16[4,6,48,128]{3,2,1,0:T(8,128)(2,1)S(1)}, bf16[4,6,48,128]{3,2,1,0:T(8,128)(2,1)S(1)}, u32[]{:S(2)}, u32[]{:S(2)}) %collective-permute-start.2) | collective-permute-done | bytes 294944 | tf_op jit(solution)/shard_map/ppermute | solution.py:123
  33.5 1.3 %collective-permute-start.3 = (bf16[4,6,48,128]{3,2,1,0:T(8,128)(2,1)S(1)}, bf16[4,6,48,128]{3,2,1,0:T(8,128)(2,1)}, u32[]{:S(2)}, u32[]{:S(2)}) collective-permute-start(bf16[4,6,48,128]{3,2,1,0:T(8,128)(2,1)S(1)} %collective-permute-done.2.refs_4_), channel_id=1, source_target_pairs={{1,0},{5,4},{9,8},{13,12},{17,16},{21,20},{25,24},{29,28},{33,32},... | collective-permute-start | bytes 884744 | tf_op jit(solution)/shard_map/ppermute | solution.py:123
  34.8 0.0 collective-permute-done.4.refs_3_
  34.8 1.4 %collective-permute-start.5 = (bf16[4,6,48,128]{3,2,1,0:T(8,128)(2,1)S(1)}, bf16[4,6,48,128]{3,2,1,0:T(8,128)(2,1)}, u32[]{:S(2)}, u32[]{:S(2)}) collective-permute-start(bf16[4,6,48,128]{3,2,1,0:T(8,128)(2,1)S(1)} %collective-permute-done.4.refs_3_), channel_id=1, source_target_pairs={{2,3},{6,7},{10,11},{14,15},{18,19},{22,23},{26,27},{30,31},{34,35... | collective-permute-start | bytes 884744 | tf_op jit(solution)/shard_map/ppermute | solution.py:122
  36.2 0.0 copy-done
  36.2 0.7 constant_dynamic-slice_fusion.1
  36.9 2.8 %copy.10 = bf16[8,6,2,128,128]{4,3,2,1,0:T(8,128)(2,1)S(1)} copy(bf16[8,6,2,128,128]{4,2,1,3,0:T(2,128)(2,1)} %bitcast.30) | data formatting | bytes 6291456 | tf_op jit(solution)/shard_map/transpose | solution.py:150
  39.7 6.4 %collective-permute-done.3.refs_2_ = bf16[4,6,48,128]{3,2,1,0:T(8,128)(2,1)} collective-permute-done((bf16[4,6,48,128]{3,2,1,0:T(8,128)(2,1)S(1)}, bf16[4,6,48,128]{3,2,1,0:T(8,128)(2,1)}, u32[]{:S(2)}, u32[]{:S(2)}) %collective-permute-start.3) | collective-permute-done | bytes 294944 | tf_op jit(solution)/shard_map/ppermute | solution.py:123
  46.1 0.0 collective-permute-done.5.refs_5_
  46.1 1.9 %forward.2 = (bf16[4,192,128]{2,1,0:T(8,128)(2,1)S(1)}, bf16[4,6,192,128]{3,2,1,0:T(8,128)(2,1)S(1)}) custom-call(bf16[4,6,48,128]{3,2,1,0:T(8,128)(2,1)S(1)} %bitcast.25, bf16[4,6,48,128]{3,2,1,0:T(8,128)(2,1)S(1)} %collective-permute-done.refs_1_, bf16[4,6,48,128]{3,2,1,0:T(8,128)(2,1)} %collective-permute-done.3.refs_2_, ...), custom_call_target="tpu_custom_call" | custom-call | flops 301989888 | bytes 2000000 | tf_op jit(solution)/shard_map/forward/pallas_call | solution.py:28
  48.0 0.0 collective-permute-done.10.refs_3_
  48.0 0.0 collective-permute-done.11.refs_6_
  48.1 0.9 forward.3
  48.9 16.8 %all_to_all.24.parts_ref = bf16[16,96,128]{2,1,0:T(8,128)(2,1)S(1)} all-to-all(bf16[16,96,128]{2,1,0:T(8,128)(2,1)S(1)} %bitcast.26), channel_id=1, replica_groups=mesh['z_far'=6,'z_near'=2,'y_hi'=2,'x'=4,'core'=2,'event'=4] {'z_near','..., dimensions={0} | all-to-all | bytes 786432 | tf_op jit(solution)/shard_map/all_to_all | solution.py:19
  65.8 0.1 near_sum.1
  65.8 35.6 %all_to_all.25.parts_ref = bf16[12,96,128]{2,1,0:T(8,128)(2,1)S(1)} all-to-all(bf16[12,96,128]{2,1,0:T(8,128)(2,1)S(1)} %near_sum.1), channel_id=1, replica_groups=mesh['z_far'=6,'z_near'=2,'y_hi'=2,'x'=4,'core'=2,'event'=4] {'z_far','y..., dimensions={0} | all-to-all | bytes 589824 | tf_op jit(solution)/shard_map/all_to_all | solution.py:19
  101.4 0.1 resid.1
  101.5 14.3 %all_to_all.26 = bf16[16,96,128]{2,1,0:T(8,128)(2,1)S(1)} all-to-all(bf16[16,96,128]{2,1,0:T(8,128)(2,1)S(1)} %resid.1), channel_id=1, replica_groups=mesh['z_far'=6,'z_near'=2,'y_hi'=2,'x'=4,'core'=2,'event'=4] {'z_near','..., dimensions={0} | all-to-all | bytes 786432 | tf_op jit(solution)/shard_map/all_to_all | solution.py:19
  115.7 2.1 %backward.1 = f32[4,32]{1,0:T(4,128)S(1)} custom-call(bf16[4,6,192,128]{3,2,1,0:T(8,128)(2,1)S(1)} %get-tuple-element.22.refs_0_, bf16[4,6,192,128]{3,2,1,0:T(8,128)(2,1)S(1)} %get-tuple-element.34.refs_1_, bf16[8,192,128]{2,1,0:T(8,128)(2,1)S(1)} %bitcast.19, bf16[8,6,256,128]{3,2,1,0:T(8,128)(2,1)S(1)} %bitcast.18), custom_call_target="tpu_custom_call" | custom-call | flops 603979776 | bytes 2000000 | tf_op jit(solution)/shard_map/backward/pallas_call | solution.py:28
  117.8 6.7 %all_to_all.27 = f32[4,1,32]{2,1,0:T(1,128)S(1)} all-to-all(f32[4,1,32]{2,1,0:T(1,128)S(1)} %bitcast.29), channel_id=1, replica_groups=mesh['z_far'=6,'z_near'=2,'y_hi'=2,'x'=4,'core'=2,'event'=4] {'event'}, dimensions={0} | all-to-all | bytes 1024 | tf_op jit(solution)/shard_map/all_to_all | solution.py:19
  124.5 0.5 broadcast_multiply_fusion
  (4 shorter events, 0.0 us)
Async XLA Ops:
  0.0 36.2 %copy-start = (f32[128]{0:T(128)S(1)}, f32[128]{0:T(128)}, u32[]{:S(2)}) copy-start(f32[128]{0:T(128)} %param.6) | copy-start | bytes 1540
  1.6 11.4 %collective-permute-start.6 = (bf16[4,6,48,128]{3,2,1,0:T(8,128)(2,1)S(1)}, bf16[4,6,48,128]{3,2,1,0:T(8,128)(2,1)S(1)}, u32[]{:S(2)}, u32[]{:S(2)}) collective-permute-start(bf16[4,6,48,128]{3,2,1,0:T(8,128)(2,1)S(1)} %bitcast.20), channel_id=1, source_target_pairs={{0,1},{1,2},{2,3},{4,5},{5,6},{6,7},{8,9},{9,10},{10,11},{12,13},{... | collective-permute-start | bytes 884744 | tf_op jit(solution)/shard_map/ppermute | solution.py:122
  5.6 8.0 %collective-permute-start.8 = (bf16[4,6,48,128]{3,2,1,0:T(8,128)(2,1)S(1)}, bf16[4,6,48,128]{3,2,1,0:T(8,128)(2,1)S(1)}, u32[]{:S(2)}, u32[]{:S(2)}) collective-permute-start(bf16[4,6,48,128]{3,2,1,0:T(8,128)(2,1)S(1)} %bitcast.21), channel_id=1, source_target_pairs={{1,0},{2,1},{3,2},{5,4},{6,5},{7,6},{9,8},{10,9},{11,10},{13,12},{... | collective-permute-start | bytes 884744 | tf_op jit(solution)/shard_map/ppermute | solution.py:123
  7.0 9.2 %collective-permute-start.1 = (bf16[4,6,48,128]{3,2,1,0:T(8,128)(2,1)S(1)}, bf16[4,6,48,128]{3,2,1,0:T(8,128)(2,1)S(1)}, u32[]{:S(2)}, u32[]{:S(2)}) collective-permute-start(bf16[4,6,48,128]{3,2,1,0:T(8,128)(2,1)S(1)} %bitcast.23), channel_id=1, source_target_pairs={{1,0},{2,1},{3,2},{5,4},{6,5},{7,6},{9,8},{10,9},{11,10},{13,12},{... | collective-permute-start | bytes 884744 | tf_op jit(solution)/shard_map/ppermute | solution.py:123
  8.3 10.9 %collective-permute-start = (bf16[4,6,48,128]{3,2,1,0:T(8,128)(2,1)S(1)}, bf16[4,6,48,128]{3,2,1,0:T(8,128)(2,1)S(1)}, u32[]{:S(2)}, u32[]{:S(2)}) collective-permute-start(bf16[4,6,48,128]{3,2,1,0:T(8,128)(2,1)S(1)} %bitcast.24), channel_id=1, source_target_pairs={{0,1},{1,2},{2,3},{4,5},{5,6},{6,7},{8,9},{9,10},{10,11},{12,13},{... | collective-permute-start | bytes 884744 | tf_op jit(solution)/shard_map/ppermute | solution.py:122
  13.0 6.9 %collective-permute-start.7 = (bf16[4,6,48,128]{3,2,1,0:T(8,128)(2,1)S(1)}, bf16[4,6,48,128]{3,2,1,0:T(8,128)(2,1)S(1)}, u32[]{:S(2)}, u32[]{:S(2)}) collective-permute-start(bf16[4,6,48,128]{3,2,1,0:T(8,128)(2,1)S(1)} %collective-permute-done.6.refs_2_), channel_id=1, source_target_pairs={{1,2},{2,3},{5,6},{6,7},{9,10},{10,11},{13,14},{14,15},{17,18},{18... | collective-permute-start | bytes 884744 | tf_op jit(solution)/shard_map/ppermute | solution.py:122
  13.7 13.5 %collective-permute-start.9 = (bf16[4,6,48,128]{3,2,1,0:T(8,128)(2,1)S(1)}, bf16[4,6,48,128]{3,2,1,0:T(8,128)(2,1)S(1)}, u32[]{:S(2)}, u32[]{:S(2)}) collective-permute-start(bf16[4,6,48,128]{3,2,1,0:T(8,128)(2,1)S(1)} %collective-permute-done.8.refs_7_), channel_id=1, source_target_pairs={{1,0},{2,1},{5,4},{6,5},{9,8},{10,9},{13,12},{14,13},{17,16},{18,1... | collective-permute-start | bytes 884744 | tf_op jit(solution)/shard_map/ppermute | solution.py:123
  16.2 17.2 %collective-permute-start.2 = (bf16[4,6,48,128]{3,2,1,0:T(8,128)(2,1)S(1)}, bf16[4,6,48,128]{3,2,1,0:T(8,128)(2,1)S(1)}, u32[]{:S(2)}, u32[]{:S(2)}) collective-permute-start(bf16[4,6,48,128]{3,2,1,0:T(8,128)(2,1)S(1)} %collective-permute-done.1.refs_6_), channel_id=1, source_target_pairs={{1,0},{2,1},{5,4},{6,5},{9,8},{10,9},{13,12},{14,13},{17,16},{18,1... | collective-permute-start | bytes 884744 | tf_op jit(solution)/shard_map/ppermute | solution.py:123
  19.2 15.6 %collective-permute-start.4 = (bf16[4,6,48,128]{3,2,1,0:T(8,128)(2,1)S(1)}, bf16[4,6,48,128]{3,2,1,0:T(8,128)(2,1)S(1)}, u32[]{:S(2)}, u32[]{:S(2)}) collective-permute-start(bf16[4,6,48,128]{3,2,1,0:T(8,128)(2,1)S(1)} %collective-permute-done.refs_1_), channel_id=1, source_target_pairs={{1,2},{2,3},{5,6},{6,7},{9,10},{10,11},{13,14},{14,15},{17,18},{18... | collective-permute-start | bytes 884744 | tf_op jit(solution)/shard_map/ppermute | solution.py:122
  27.2 20.9 %collective-permute-start.10 = (bf16[4,6,48,128]{3,2,1,0:T(8,128)(2,1)S(1)}, bf16[4,6,48,128]{3,2,1,0:T(8,128)(2,1)S(1)}, u32[]{:S(2)}, u32[]{:S(2)}) collective-permute-start(bf16[4,6,48,128]{3,2,1,0:T(8,128)(2,1)S(1)} %collective-permute-done.9.refs_5_), channel_id=1, source_target_pairs={{1,0},{5,4},{9,8},{13,12},{17,16},{21,20},{25,24},{29,28},{33,32},... | collective-permute-start | bytes 884744 | tf_op jit(solution)/shard_map/ppermute | solution.py:123
  28.5 19.6 %collective-permute-start.11 = (bf16[4,6,48,128]{3,2,1,0:T(8,128)(2,1)S(1)}, bf16[4,6,48,128]{3,2,1,0:T(8,128)(2,1)S(1)}, u32[]{:S(2)}, u32[]{:S(2)}) collective-permute-start(bf16[4,6,48,128]{3,2,1,0:T(8,128)(2,1)S(1)} %collective-permute-done.7.refs_4_), channel_id=1, source_target_pairs={{2,3},{6,7},{10,11},{14,15},{18,19},{22,23},{26,27},{30,31},{34,35... | collective-permute-start | bytes 884744 | tf_op jit(solution)/shard_map/ppermute | solution.py:122
  33.5 12.6 %collective-permute-start.3 = (bf16[4,6,48,128]{3,2,1,0:T(8,128)(2,1)S(1)}, bf16[4,6,48,128]{3,2,1,0:T(8,128)(2,1)}, u32[]{:S(2)}, u32[]{:S(2)}) collective-permute-start(bf16[4,6,48,128]{3,2,1,0:T(8,128)(2,1)S(1)} %collective-permute-done.2.refs_4_), channel_id=1, source_target_pairs={{1,0},{5,4},{9,8},{13,12},{17,16},{21,20},{25,24},{29,28},{33,32},... | collective-permute-start | bytes 884744 | tf_op jit(solution)/shard_map/ppermute | solution.py:123
  34.8 11.3 %collective-permute-start.5 = (bf16[4,6,48,128]{3,2,1,0:T(8,128)(2,1)S(1)}, bf16[4,6,48,128]{3,2,1,0:T(8,128)(2,1)}, u32[]{:S(2)}, u32[]{:S(2)}) collective-permute-start(bf16[4,6,48,128]{3,2,1,0:T(8,128)(2,1)S(1)} %collective-permute-done.4.refs_3_), channel_id=1, source_target_pairs={{2,3},{6,7},{10,11},{14,15},{18,19},{22,23},{26,27},{30,31},{34,35... | collective-permute-start | bytes 884744 | tf_op jit(solution)/shard_map/ppermute | solution.py:122

commit v3 on v2

--- a/solution.py
+++ b/solution.py
@@ -11,7 +11,7 @@
 PIECES = 2
 SPACE = ("z_far", "z_near", "y_hi", "x", "core")
 NEAR = ("z_near", "x", "core")
-FAR = ("z_far", "y_hi")
+FAR = ("z_far",)
 WHOLE = pl.BlockSpec(memory_space=pltpu.VMEM)
 
 
@@ -76,10 +76,15 @@
         out_ref[i] = total
 
 
-def resid_kernel(scale, own, parts_ref, pairs_ref, out_ref):
+def far_sum_kernel(parts_ref, out_ref):
     total = parts_ref[0].astype(jnp.float32)
     for i in range(1, parts_ref.shape[0]):
         total = total + parts_ref[i].astype(jnp.float32)
+    out_ref[...] = total
+
+
+def resid_kernel(scale, own, mine_ref, other_ref, pairs_ref, out_ref):
+    total = mine_ref[...] + other_ref[...]
     mask = pairs_ref[...].astype(jnp.float32)
     mask = [mask[j:j + own] for j in range(0, mask.shape[0], own)]
     mask = jnp.concatenate([m for m in mask for _ in range(2)], 0)
@@ -135,17 +140,21 @@
     n_rows = 2 * events
     share = freqs // PIECES
     tall = freqs * n_rows // near
-    scale_one = 1.0 / math.sqrt(12.0 * cells * near * far)
+    scale_one = 1.0 / math.sqrt(12.0 * cells * near * far * lax.axis_size("y_hi"))
     scale_two = 1.0 / math.sqrt(12.0 * events * freqs * recv * n_event)
     bf16 = functools.partial(jax.ShapeDtypeStruct, dtype=jnp.bfloat16)
 
-    mine = strain.transpose(1, 3, 2, 0, 4).reshape(freqs, comps, 2 * own, cells)
-    pieces = [mine[h * share:(h + 1) * share] for h in range(PIECES)]
+    pieces = []
+    for h in range(PIECES):
+        if h > 0:
+            pieces[-1], strain = lax.optimization_barrier((pieces[-1], strain))
+        part = strain[:, h * share:(h + 1) * share]
+        pieces.append(part.transpose(1, 3, 2, 0, 4).reshape(share, comps, 2 * own, cells))
     hops = [hop([(p, p) for p in pieces], 1)]
     for k in range(2, n_event):
         if k == n_event - 1:
-            last, green = lax.optimization_barrier((hops[-1][-1], green))
-            hops[-1][-1] = last
+            early, green = lax.optimization_barrier((hops[-1][0], green))
+            hops[-1][0] = early
         hops.append(hop(hops[-1], k))
     flat_green = green.transpose(0, 3, 2, 1, 4).reshape(freqs, comps, 2 * recv, cells)
 
@@ -176,8 +185,10 @@
 
     got = exchange(partial.reshape(near, tall, recv), NEAR)
     summed = exchange(call(near_sum_kernel, "near_sum", 0, bf16((far, tall, recv)), got), FAR)
+    summed = call(far_sum_kernel, "far_sum", 0, jax.ShapeDtypeStruct((tall, recv), jnp.float32), summed)
+    other = lax.ppermute(summed, "y_hi", [(0, 1), (1, 0)])
     resid = call(
-        functools.partial(resid_kernel, scale_one, own), "resid", 0, bf16((near, tall, recv)), summed, recorded
+        functools.partial(resid_kernel, scale_one, own), "resid", 0, bf16((near, tall, recv)), summed, other, recorded
     )
     resid = exchange(resid, NEAR).reshape(freqs, n_rows, recv)
     local_cells = call(

time: 126 us -> 123 us (0.976)
  blocking collectives: 73.4 us -> 65 us
  starting transfers between devices: 19.8 us -> 26.4 us
  waiting for transfers between devices: 21 us -> 19.4 us
    all_to_all x4, blocking collectives: 73.4 us -> 65 us  [exchange(): return lax.all_to_all(parts, axes, 0, 0, tiled=True)]
    ppermute x0 -> x1, starting transfers between devices: none -> 6.55 us  [body(): other = lax.ppermute(summed, 'y_hi', [(0, 1), (1, 0)])]
    ppermute x6, waiting for transfers between devices: 19.4 us -> 14.4 us  [hop(): lax.ppermute(down, 'event', [(i, i - 1) for i in range(1, n + 1 - k)])]
    transpose x0 -> x4, local copies, waits for them, and re-layouts: none -> 2.51 us  [body(): part.transpose(1, 3, 2, 0, 4).reshape(share, comps, 2 * own, cells)]
    ppermute x0 -> x1, waiting for transfers between devices: none -> 2.18 us  [body(): other = lax.ppermute(summed, 'y_hi', [(0, 1), (1, 0)])]
    slice x3 -> x0, local copies, waits for them, and re-layouts: 1.63 us -> none  [body(): pieces = [mine[h * share:(h + 1) * share] for h in range(PIECES)]]
    pallas_call x5 -> x6, Pallas kernels: 4.95 us -> 4.96 us  [call(): pl.pallas_call(kernel, in_specs=[WHOLE] * len(args), out_specs=WHOLE if s...]
  transfers between devices with their start and end apart: 12 -> 13, of which waited for: 5 -> 7; matrix products, arithmetic and copies ran while one was open for 3% -> 4% of each run, Pallas kernels for 2% -> 2%
where the time goes in v3:
time: 123 us
  blocking collectives  65 us (53%)
  starting transfers between devices  26.4 us (21%)
  waiting for transfers between devices  19.4 us (16%)
  local copies, waits for them, and re-layouts  6.01 us (5%)
  Pallas kernels  4.96 us (4%)
    all_to_all x4, blocking collectives, exchange(): return lax.all_to_all(parts, axes, 0, 0, tiled=True)  65 us
    ppermute x6, waiting for transfers between devices, hop(): lax.ppermute(down, 'event', [(i, i - 1) for i in range(1, n + 1 - k)])  14.4 us
    ppermute x6, starting transfers between devices, hop(): lax.ppermute(up, 'event', [(i, i + 1) for i in range(k - 1, n - 1)])  12.1 us
    ppermute x6, starting transfers between devices, hop(): lax.ppermute(down, 'event', [(i, i - 1) for i in range(1, n + 1 - k)])  7.72 us
    ppermute x1, starting transfers between devices, body(): other = lax.ppermute(summed, 'y_hi', [(0, 1), (1, 0)])  6.55 us
    pallas_call x6, Pallas kernels, call(): pl.pallas_call(kernel, in_specs=[WHOLE] * len(args), out_specs=WHOLE if s...  4.96 us
    ppermute x6, waiting for transfers between devices, hop(): lax.ppermute(up, 'event', [(i, i + 1) for i in range(k - 1, n - 1)])  2.81 us
    transpose x1, local copies, waits for them, and re-layouts, body(): green.transpose(0, 3, 2, 1, 4).reshape(freqs, comps, 2 * recv, cells)  2.76 us
  transfers between devices with their start and end apart: 13, of which 7 were waited for; matrix products, arithmetic and copies ran while one was open for 4% of the time, Pallas kernels for 2%

profile of v3, /device:TPU:1, one launch (start us, length us, event | category | flops | bytes accessed | tf_op | source)
XLA Modules:
  0.0 122.5 jit_solution(7641067785085699743)
XLA Ops:
  0.0 0.0 copy-start
  0.0 1.2 slice_bitcast_fusion.1
  1.2 0.1 copy.8
  1.3 4.0 %collective-permute-start = (bf16[4,6,48,128]{3,2,1,0:T(8,128)(2,1)S(1)}, bf16[4,6,48,128]{3,2,1,0:T(8,128)(2,1)S(1)}, u32[]{:S(2)}, u32[]{:S(2)}) collective-permute-start(bf16[4,6,48,128]{3,2,1,0:T(8,128)(2,1)S(1)} %bitcast.26), channel_id=1, source_target_pairs={{0,1},{1,2},{2,3},{4,5},{5,6},{6,7},{8,9},{9,10},{10,11},{12,13},{... | collective-permute-start | bytes 884744 | tf_op jit(solution)/shard_map/ppermute | solution.py:127
  5.3 1.3 %collective-permute-start.2 = (bf16[4,6,48,128]{3,2,1,0:T(8,128)(2,1)S(1)}, bf16[4,6,48,128]{3,2,1,0:T(8,128)(2,1)S(1)}, u32[]{:S(2)}, u32[]{:S(2)}) collective-permute-start(bf16[4,6,48,128]{3,2,1,0:T(8,128)(2,1)S(1)} %bitcast.27), channel_id=1, source_target_pairs={{1,0},{2,1},{3,2},{5,4},{6,5},{7,6},{9,8},{10,9},{11,10},{13,12},{... | collective-permute-start | bytes 884744 | tf_op jit(solution)/shard_map/ppermute | solution.py:128
  6.6 1.2 slice_bitcast_fusion
  7.8 0.1 copy.10
  7.9 1.3 %collective-permute-start.7 = (bf16[4,6,48,128]{3,2,1,0:T(8,128)(2,1)S(1)}, bf16[4,6,48,128]{3,2,1,0:T(8,128)(2,1)S(1)}, u32[]{:S(2)}, u32[]{:S(2)}) collective-permute-start(bf16[4,6,48,128]{3,2,1,0:T(8,128)(2,1)S(1)} %bitcast.23), channel_id=1, source_target_pairs={{1,0},{2,1},{3,2},{5,4},{6,5},{7,6},{9,8},{10,9},{11,10},{13,12},{... | collective-permute-start | bytes 884744 | tf_op jit(solution)/shard_map/ppermute | solution.py:128
  9.2 4.6 %collective-permute-start.6 = (bf16[4,6,48,128]{3,2,1,0:T(8,128)(2,1)S(1)}, bf16[4,6,48,128]{3,2,1,0:T(8,128)(2,1)S(1)}, u32[]{:S(2)}, u32[]{:S(2)}) collective-permute-start(bf16[4,6,48,128]{3,2,1,0:T(8,128)(2,1)S(1)} %bitcast.24), channel_id=1, source_target_pairs={{0,1},{1,2},{2,3},{4,5},{5,6},{6,7},{8,9},{9,10},{10,11},{12,13},{... | collective-permute-start | bytes 884744 | tf_op jit(solution)/shard_map/ppermute | solution.py:127
  13.8 0.0 collective-permute-done.refs_1_
  13.8 0.7 collective-permute-start.1
  14.5 0.0 collective-permute-done.2.refs_6_
  14.5 1.3 %collective-permute-start.3 = (bf16[4,6,48,128]{3,2,1,0:T(8,128)(2,1)S(1)}, bf16[4,6,48,128]{3,2,1,0:T(8,128)(2,1)S(1)}, u32[]{:S(2)}, u32[]{:S(2)}) collective-permute-start(bf16[4,6,48,128]{3,2,1,0:T(8,128)(2,1)S(1)} %collective-permute-done.2.refs_6_), channel_id=1, source_target_pairs={{1,0},{2,1},{5,4},{6,5},{9,8},{10,9},{13,12},{14,13},{17,16},{18,1... | collective-permute-start | bytes 884744 | tf_op jit(solution)/shard_map/ppermute | solution.py:128
  15.8 0.1 collective-permute-done.7.refs_7_
  16.0 1.3 %collective-permute-start.8 = (bf16[4,6,48,128]{3,2,1,0:T(8,128)(2,1)S(1)}, bf16[4,6,48,128]{3,2,1,0:T(8,128)(2,1)S(1)}, u32[]{:S(2)}, u32[]{:S(2)}) collective-permute-start(bf16[4,6,48,128]{3,2,1,0:T(8,128)(2,1)S(1)} %collective-permute-done.7.refs_7_), channel_id=1, source_target_pairs={{1,0},{2,1},{5,4},{6,5},{9,8},{10,9},{13,12},{14,13},{17,16},{18,1... | collective-permute-start | bytes 884744 | tf_op jit(solution)/shard_map/ppermute | solution.py:128
  17.3 2.8 %collective-permute-done.6.refs_2_ = bf16[4,6,48,128]{3,2,1,0:T(8,128)(2,1)S(1)} collective-permute-done((bf16[4,6,48,128]{3,2,1,0:T(8,128)(2,1)S(1)}, bf16[4,6,48,128]{3,2,1,0:T(8,128)(2,1)S(1)}, u32[]{:S(2)}, u32[]{:S(2)}) %collective-permute-start.6) | collective-permute-done | bytes 294944 | tf_op jit(solution)/shard_map/ppermute | solution.py:127
  20.1 0.7 collective-permute-start.10
  20.8 0.0 collective-permute-done.1.refs_3_
  20.8 6.6 %collective-permute-done.3.refs_4_ = bf16[4,6,48,128]{3,2,1,0:T(8,128)(2,1)S(1)} collective-permute-done((bf16[4,6,48,128]{3,2,1,0:T(8,128)(2,1)S(1)}, bf16[4,6,48,128]{3,2,1,0:T(8,128)(2,1)S(1)}, u32[]{:S(2)}, u32[]{:S(2)}) %collective-permute-start.3) | collective-permute-done | bytes 294944 | tf_op jit(solution)/shard_map/ppermute | solution.py:128
  27.4 1.3 %collective-permute-start.4 = (bf16[4,6,48,128]{3,2,1,0:T(8,128)(2,1)S(1)}, bf16[4,6,48,128]{3,2,1,0:T(8,128)(2,1)}, u32[]{:S(2)}, u32[]{:S(2)}) collective-permute-start(bf16[4,6,48,128]{3,2,1,0:T(8,128)(2,1)S(1)} %collective-permute-done.3.refs_4_), channel_id=1, source_target_pairs={{1,0},{5,4},{9,8},{13,12},{17,16},{21,20},{25,24},{29,28},{33,32},... | collective-permute-start | bytes 884744 | tf_op jit(solution)/shard_map/ppermute | solution.py:128
  28.7 1.4 %collective-permute-start.5 = (bf16[4,6,48,128]{3,2,1,0:T(8,128)(2,1)S(1)}, bf16[4,6,48,128]{3,2,1,0:T(8,128)(2,1)}, u32[]{:S(2)}, u32[]{:S(2)}) collective-permute-start(bf16[4,6,48,128]{3,2,1,0:T(8,128)(2,1)S(1)} %collective-permute-done.1.refs_3_), channel_id=1, source_target_pairs={{2,3},{6,7},{10,11},{14,15},{18,19},{22,23},{26,27},{30,31},{34,35... | collective-permute-start | bytes 884744 | tf_op jit(solution)/shard_map/ppermute | solution.py:127
  30.1 2.4 %collective-permute-done.8.refs_5_ = bf16[4,6,48,128]{3,2,1,0:T(8,128)(2,1)S(1)} collective-permute-done((bf16[4,6,48,128]{3,2,1,0:T(8,128)(2,1)S(1)}, bf16[4,6,48,128]{3,2,1,0:T(8,128)(2,1)S(1)}, u32[]{:S(2)}, u32[]{:S(2)}) %collective-permute-start.8) | collective-permute-done | bytes 294944 | tf_op jit(solution)/shard_map/ppermute | solution.py:128
  32.4 1.3 %collective-permute-start.9 = (bf16[4,6,48,128]{3,2,1,0:T(8,128)(2,1)S(1)}, bf16[4,6,48,128]{3,2,1,0:T(8,128)(2,1)S(1)}, u32[]{:S(2)}, u32[]{:S(2)}) collective-permute-start(bf16[4,6,48,128]{3,2,1,0:T(8,128)(2,1)S(1)} %collective-permute-done.8.refs_5_), channel_id=1, source_target_pairs={{1,0},{5,4},{9,8},{13,12},{17,16},{21,20},{25,24},{29,28},{33,32},... | collective-permute-start | bytes 884744 | tf_op jit(solution)/shard_map/ppermute | solution.py:128
  33.7 0.0 collective-permute-done.10.refs_4_
  33.7 0.7 collective-permute-start.11
  34.4 0.0 copy-done
  34.5 0.7 constant_dynamic-slice_fusion.1
  35.3 2.8 %copy.9 = bf16[8,6,2,128,128]{4,3,2,1,0:T(8,128)(2,1)S(1)} copy(bf16[8,6,2,128,128]{4,2,1,3,0:T(2,128)(2,1)} %bitcast.33) | data formatting | bytes 6291456 | tf_op jit(solution)/shard_map/transpose | solution.py:159
  38.0 0.7 collective-permute-done.4.refs_2_
  38.8 0.0 collective-permute-done.5.refs_5_
  38.8 1.9 %forward.2 = (bf16[4,192,128]{2,1,0:T(8,128)(2,1)S(1)}, bf16[4,6,192,128]{3,2,1,0:T(8,128)(2,1)S(1)}) custom-call(bf16[4,6,48,128]{3,2,1,0:T(8,128)(2,1)S(1)} %bitcast.28, bf16[4,6,48,128]{3,2,1,0:T(8,128)(2,1)S(1)} %collective-permute-done.refs_1_, bf16[4,6,48,128]{3,2,1,0:T(8,128)(2,1)} %collective-permute-done.4.refs_2_, ...), custom_call_target="tpu_custom_call" | custom-call | flops 301989888 | bytes 2000000 | tf_op jit(solution)/shard_map/forward/pallas_call | solution.py:28
  40.7 4.5 %collective-permute-done.9.refs_3_ = bf16[4,6,48,128]{3,2,1,0:T(8,128)(2,1)S(1)} collective-permute-done((bf16[4,6,48,128]{3,2,1,0:T(8,128)(2,1)S(1)}, bf16[4,6,48,128]{3,2,1,0:T(8,128)(2,1)S(1)}, u32[]{:S(2)}, u32[]{:S(2)}) %collective-permute-start.9) | collective-permute-done | bytes 294944 | tf_op jit(solution)/shard_map/ppermute | solution.py:128
  45.2 0.0 collective-permute-done.11.refs_6_
  45.2 0.9 forward.3
  46.1 17.4 %all_to_all.24.parts_ref = bf16[16,96,128]{2,1,0:T(8,128)(2,1)S(1)} all-to-all(bf16[16,96,128]{2,1,0:T(8,128)(2,1)S(1)} %bitcast.29), channel_id=1, replica_groups=mesh['z_far'=6,'z_near'=2,'y_hi'=2,'x'=4,'core'=2,'event'=4] {'z_near','..., dimensions={0} | all-to-all | bytes 786432 | tf_op jit(solution)/shard_map/all_to_all | solution.py:19
  63.4 0.1 near_sum.1
  63.5 23.3 %all_to_all.25.parts_ref = bf16[6,96,128]{2,1,0:T(8,128)(2,1)S(1)} all-to-all(bf16[6,96,128]{2,1,0:T(8,128)(2,1)S(1)} %near_sum.1), channel_id=1, replica_groups=mesh['z_far'=6,'z_near'=2,'y_hi'=2,'x'=4,'core'=2,'event'=4] {'z_far'}, dimensions={0} | all-to-all | bytes 294912 | tf_op jit(solution)/shard_map/all_to_all | solution.py:19
  86.8 6.6 %collective-permute-start.12 = (f32[96,128]{1,0:T(8,128)S(1)}, f32[96,128]{1,0:T(8,128)S(1)}, u32[]{:S(2)}, u32[]{:S(2)}) collective-permute-start(f32[96,128]{1,0:T(8,128)S(1)} %far_sum.1.mine_ref), channel_id=1, source_target_pairs={{0,32},{32,0},{1,33},{33,1},{2,34},{34,2},{3,35},{35,3},{4,36},{36... | collective-permute-start | bytes 147464 | tf_op jit(solution)/shard_map/ppermute | solution.py:189
  93.4 2.2 %collective-permute-done.12.other_ref = f32[96,128]{1,0:T(8,128)S(1)} collective-permute-done((f32[96,128]{1,0:T(8,128)S(1)}, f32[96,128]{1,0:T(8,128)S(1)}, u32[]{:S(2)}, u32[]{:S(2)}) %collective-permute-start.12) | collective-permute-done | bytes 49184 | tf_op jit(solution)/shard_map/ppermute | solution.py:189
  95.6 16.4 %all_to_all.26 = bf16[16,96,128]{2,1,0:T(8,128)(2,1)S(1)} all-to-all(bf16[16,96,128]{2,1,0:T(8,128)(2,1)S(1)} %resid.1), channel_id=1, replica_groups=mesh['z_far'=6,'z_near'=2,'y_hi'=2,'x'=4,'core'=2,'event'=4] {'z_near','..., dimensions={0} | all-to-all | bytes 786432 | tf_op jit(solution)/shard_map/all_to_all | solution.py:19
  112.0 2.1 %backward.1 = f32[4,32]{1,0:T(4,128)S(1)} custom-call(bf16[4,6,192,128]{3,2,1,0:T(8,128)(2,1)S(1)} %get-tuple-element.27.refs_0_, bf16[4,6,192,128]{3,2,1,0:T(8,128)(2,1)S(1)} %get-tuple-element.38.refs_1_, bf16[8,192,128]{2,1,0:T(8,128)(2,1)S(1)} %bitcast.22, bf16[8,6,256,128]{3,2,1,0:T(8,128)(2,1)S(1)} %bitcast.21), custom_call_target="tpu_custom_call" | custom-call | flops 603979776 | bytes 2000000 | tf_op jit(solution)/shard_map/backward/pallas_call | solution.py:28
  114.1 7.9 %all_to_all.27 = f32[4,1,32]{2,1,0:T(1,128)S(1)} all-to-all(f32[4,1,32]{2,1,0:T(1,128)S(1)} %bitcast.32), channel_id=1, replica_groups=mesh['z_far'=6,'z_near'=2,'y_hi'=2,'x'=4,'core'=2,'event'=4] {'event'}, dimensions={0} | all-to-all | bytes 1024 | tf_op jit(solution)/shard_map/all_to_all | solution.py:19
  122.0 0.5 broadcast_multiply_fusion
  (6 shorter events, 0.1 us)
Async XLA Ops:
  0.0 34.4 %copy-start = (f32[128]{0:T(128)S(1)}, f32[128]{0:T(128)}, u32[]{:S(2)}) copy-start(f32[128]{0:T(128)} %param.6) | copy-start | bytes 1540
  1.3 12.6 %collective-permute-start = (bf16[4,6,48,128]{3,2,1,0:T(8,128)(2,1)S(1)}, bf16[4,6,48,128]{3,2,1,0:T(8,128)(2,1)S(1)}, u32[]{:S(2)}, u32[]{:S(2)}) collective-permute-start(bf16[4,6,48,128]{3,2,1,0:T(8,128)(2,1)S(1)} %bitcast.26), channel_id=1, source_target_pairs={{0,1},{1,2},{2,3},{4,5},{5,6},{6,7},{8,9},{9,10},{10,11},{12,13},{... | collective-permute-start | bytes 884744 | tf_op jit(solution)/shard_map/ppermute | solution.py:127
  5.3 9.2 %collective-permute-start.2 = (bf16[4,6,48,128]{3,2,1,0:T(8,128)(2,1)S(1)}, bf16[4,6,48,128]{3,2,1,0:T(8,128)(2,1)S(1)}, u32[]{:S(2)}, u32[]{:S(2)}) collective-permute-start(bf16[4,6,48,128]{3,2,1,0:T(8,128)(2,1)S(1)} %bitcast.27), channel_id=1, source_target_pairs={{1,0},{2,1},{3,2},{5,4},{6,5},{7,6},{9,8},{10,9},{11,10},{13,12},{... | collective-permute-start | bytes 884744 | tf_op jit(solution)/shard_map/ppermute | solution.py:128
  7.9 8.1 %collective-permute-start.7 = (bf16[4,6,48,128]{3,2,1,0:T(8,128)(2,1)S(1)}, bf16[4,6,48,128]{3,2,1,0:T(8,128)(2,1)S(1)}, u32[]{:S(2)}, u32[]{:S(2)}) collective-permute-start(bf16[4,6,48,128]{3,2,1,0:T(8,128)(2,1)S(1)} %bitcast.23), channel_id=1, source_target_pairs={{1,0},{2,1},{3,2},{5,4},{6,5},{7,6},{9,8},{10,9},{11,10},{13,12},{... | collective-permute-start | bytes 884744 | tf_op jit(solution)/shard_map/ppermute | solution.py:128
  9.2 10.9 %collective-permute-start.6 = (bf16[4,6,48,128]{3,2,1,0:T(8,128)(2,1)S(1)}, bf16[4,6,48,128]{3,2,1,0:T(8,128)(2,1)S(1)}, u32[]{:S(2)}, u32[]{:S(2)}) collective-permute-start(bf16[4,6,48,128]{3,2,1,0:T(8,128)(2,1)S(1)} %bitcast.24), channel_id=1, source_target_pairs={{0,1},{1,2},{2,3},{4,5},{5,6},{6,7},{8,9},{9,10},{10,11},{12,13},{... | collective-permute-start | bytes 884744 | tf_op jit(solution)/shard_map/ppermute | solution.py:127
  13.8 6.9 %collective-permute-start.1 = (bf16[4,6,48,128]{3,2,1,0:T(8,128)(2,1)S(1)}, bf16[4,6,48,128]{3,2,1,0:T(8,128)(2,1)S(1)}, u32[]{:S(2)}, u32[]{:S(2)}) collective-permute-start(bf16[4,6,48,128]{3,2,1,0:T(8,128)(2,1)S(1)} %collective-permute-done.refs_1_), channel_id=1, source_target_pairs={{1,2},{2,3},{5,6},{6,7},{9,10},{10,11},{13,14},{14,15},{17,18},{18... | collective-permute-start | bytes 884744 | tf_op jit(solution)/shard_map/ppermute | solution.py:127
  14.5 12.8 %collective-permute-start.3 = (bf16[4,6,48,128]{3,2,1,0:T(8,128)(2,1)S(1)}, bf16[4,6,48,128]{3,2,1,0:T(8,128)(2,1)S(1)}, u32[]{:S(2)}, u32[]{:S(2)}) collective-permute-start(bf16[4,6,48,128]{3,2,1,0:T(8,128)(2,1)S(1)} %collective-permute-done.2.refs_6_), channel_id=1, source_target_pairs={{1,0},{2,1},{5,4},{6,5},{9,8},{10,9},{13,12},{14,13},{17,16},{18,1... | collective-permute-start | bytes 884744 | tf_op jit(solution)/shard_map/ppermute | solution.py:128
  16.0 16.4 %collective-permute-start.8 = (bf16[4,6,48,128]{3,2,1,0:T(8,128)(2,1)S(1)}, bf16[4,6,48,128]{3,2,1,0:T(8,128)(2,1)S(1)}, u32[]{:S(2)}, u32[]{:S(2)}) collective-permute-start(bf16[4,6,48,128]{3,2,1,0:T(8,128)(2,1)S(1)} %collective-permute-done.7.refs_7_), channel_id=1, source_target_pairs={{1,0},{2,1},{5,4},{6,5},{9,8},{10,9},{13,12},{14,13},{17,16},{18,1... | collective-permute-start | bytes 884744 | tf_op jit(solution)/shard_map/ppermute | solution.py:128
  20.1 13.6 %collective-permute-start.10 = (bf16[4,6,48,128]{3,2,1,0:T(8,128)(2,1)S(1)}, bf16[4,6,48,128]{3,2,1,0:T(8,128)(2,1)S(1)}, u32[]{:S(2)}, u32[]{:S(2)}) collective-permute-start(bf16[4,6,48,128]{3,2,1,0:T(8,128)(2,1)S(1)} %collective-permute-done.6.refs_2_), channel_id=1, source_target_pairs={{1,2},{2,3},{5,6},{6,7},{9,10},{10,11},{13,14},{14,15},{17,18},{18... | collective-permute-start | bytes 884744 | tf_op jit(solution)/shard_map/ppermute | solution.py:127
  27.4 11.4 %collective-permute-start.4 = (bf16[4,6,48,128]{3,2,1,0:T(8,128)(2,1)S(1)}, bf16[4,6,48,128]{3,2,1,0:T(8,128)(2,1)}, u32[]{:S(2)}, u32[]{:S(2)}) collective-permute-start(bf16[4,6,48,128]{3,2,1,0:T(8,128)(2,1)S(1)} %collective-permute-done.3.refs_4_), channel_id=1, source_target_pairs={{1,0},{5,4},{9,8},{13,12},{17,16},{21,20},{25,24},{29,28},{33,32},... | collective-permute-start | bytes 884744 | tf_op jit(solution)/shard_map/ppermute | solution.py:128
  28.7 10.1 %collective-permute-start.5 = (bf16[4,6,48,128]{3,2,1,0:T(8,128)(2,1)S(1)}, bf16[4,6,48,128]{3,2,1,0:T(8,128)(2,1)}, u32[]{:S(2)}, u32[]{:S(2)}) collective-permute-start(bf16[4,6,48,128]{3,2,1,0:T(8,128)(2,1)S(1)} %collective-permute-done.1.refs_3_), channel_id=1, source_target_pairs={{2,3},{6,7},{10,11},{14,15},{18,19},{22,23},{26,27},{30,31},{34,35... | collective-permute-start | bytes 884744 | tf_op jit(solution)/shard_map/ppermute | solution.py:127
  32.4 12.7 %collective-permute-start.9 = (bf16[4,6,48,128]{3,2,1,0:T(8,128)(2,1)S(1)}, bf16[4,6,48,128]{3,2,1,0:T(8,128)(2,1)S(1)}, u32[]{:S(2)}, u32[]{:S(2)}) collective-permute-start(bf16[4,6,48,128]{3,2,1,0:T(8,128)(2,1)S(1)} %collective-permute-done.8.refs_5_), channel_id=1, source_target_pairs={{1,0},{5,4},{9,8},{13,12},{17,16},{21,20},{25,24},{29,28},{33,32},... | collective-permute-start | bytes 884744 | tf_op jit(solution)/shard_map/ppermute | solution.py:128
  33.7 11.4 %collective-permute-start.11 = (bf16[4,6,48,128]{3,2,1,0:T(8,128)(2,1)S(1)}, bf16[4,6,48,128]{3,2,1,0:T(8,128)(2,1)S(1)}, u32[]{:S(2)}, u32[]{:S(2)}) collective-permute-start(bf16[4,6,48,128]{3,2,1,0:T(8,128)(2,1)S(1)} %collective-permute-done.10.refs_4_), channel_id=1, source_target_pairs={{2,3},{6,7},{10,11},{14,15},{18,19},{22,23},{26,27},{30,31},{34,35... | collective-permute-start | bytes 884744 | tf_op jit(solution)/shard_map/ppermute | solution.py:127
  86.8 8.7 %collective-permute-start.12 = (f32[96,128]{1,0:T(8,128)S(1)}, f32[96,128]{1,0:T(8,128)S(1)}, u32[]{:S(2)}, u32[]{:S(2)}) collective-permute-start(f32[96,128]{1,0:T(8,128)S(1)} %far_sum.1.mine_ref), channel_id=1, source_target_pairs={{0,32},{32,0},{1,33},{33,1},{2,34},{34,2},{3,35},{35,3},{4,36},{36... | collective-permute-start | bytes 147464 | tf_op jit(solution)/shard_map/ppermute | solution.py:189

commit v4 on v3

--- a/solution.py
+++ b/solution.py
@@ -76,15 +76,16 @@
         out_ref[i] = total
 
 
-def far_sum_kernel(parts_ref, out_ref):
+def far_sum_kernel(parts_ref, out_ref, send_ref):
     total = parts_ref[0].astype(jnp.float32)
     for i in range(1, parts_ref.shape[0]):
         total = total + parts_ref[i].astype(jnp.float32)
     out_ref[...] = total
+    send_ref[...] = total.astype(send_ref.dtype)
 
 
 def resid_kernel(scale, own, mine_ref, other_ref, pairs_ref, out_ref):
-    total = mine_ref[...] + other_ref[...]
+    total = mine_ref[...] + other_ref[...].astype(jnp.float32)
     mask = pairs_ref[...].astype(jnp.float32)
     mask = [mask[j:j + own] for j in range(0, mask.shape[0], own)]
     mask = jnp.concatenate([m for m in mask for _ in range(2)], 0)
@@ -185,8 +186,9 @@
 
     got = exchange(partial.reshape(near, tall, recv), NEAR)
     summed = exchange(call(near_sum_kernel, "near_sum", 0, bf16((far, tall, recv)), got), FAR)
-    summed = call(far_sum_kernel, "far_sum", 0, jax.ShapeDtypeStruct((tall, recv), jnp.float32), summed)
-    other = lax.ppermute(summed, "y_hi", [(0, 1), (1, 0)])
+    outs = [jax.ShapeDtypeStruct((tall, recv), jnp.float32), bf16((tall, recv))]
+    summed, sent = call(far_sum_kernel, "far_sum", 0, outs, summed)
+    other = lax.ppermute(sent, "y_hi", [(0, 1), (1, 0)])
     resid = call(
         functools.partial(resid_kernel, scale_one, own), "resid", 0, bf16((near, tall, recv)), summed, other, recorded
     )

time: 123 us -> 123 us (level)
  no operation moved by 1% of the time
where the time goes in v4:
time: 123 us; the launch traced here: 122 us
  blocking collectives  65 us (53%)
  starting transfers between devices  26.4 us (21%)
  waiting for transfers between devices  19.1 us (16%)
  local copies, waits for them, and re-layouts  6.01 us (5%)
  Pallas kernels  4.96 us (4%)
    all_to_all x4, blocking collectives, exchange(): return lax.all_to_all(parts, axes, 0, 0, tiled=True)  65 us
    ppermute x6, waiting for transfers between devices, hop(): lax.ppermute(down, 'event', [(i, i - 1) for i in range(1, n + 1 - k)])  14.4 us
    ppermute x6, starting transfers between devices, hop(): lax.ppermute(up, 'event', [(i, i + 1) for i in range(k - 1, n - 1)])  12.1 us
    ppermute x6, starting transfers between devices, hop(): lax.ppermute(down, 'event', [(i, i - 1) for i in range(1, n + 1 - k)])  7.72 us
    ppermute x1, starting transfers between devices, body(): other = lax.ppermute(sent, 'y_hi', [(0, 1), (1, 0)])  6.55 us
    pallas_call x6, Pallas kernels, call(): pl.pallas_call(kernel, in_specs=[WHOLE] * len(args), out_specs=WHOLE if s...  4.96 us
    ppermute x6, waiting for transfers between devices, hop(): lax.ppermute(up, 'event', [(i, i + 1) for i in range(k - 1, n - 1)])  2.81 us
    transpose x1, local copies, waits for them, and re-layouts, body(): green.transpose(0, 3, 2, 1, 4).reshape(freqs, comps, 2 * recv, cells)  2.76 us
  transfers between devices with their start and end apart: 13, of which 7 were waited for; matrix products, arithmetic and copies ran while one was open for 4% of the time, Pallas kernels for 2%

profile of v4, /device:TPU:1, one launch (start us, length us, event | category | flops | bytes accessed | tf_op | source)
XLA Modules:
  0.0 122.3 jit_solution(840967229242747024)
XLA Ops:
  0.0 0.0 copy-start
  0.0 1.2 slice_bitcast_fusion.1
  1.2 0.1 copy.8
  1.3 4.0 %collective-permute-start = (bf16[4,6,48,128]{3,2,1,0:T(8,128)(2,1)S(1)}, bf16[4,6,48,128]{3,2,1,0:T(8,128)(2,1)S(1)}, u32[]{:S(2)}, u32[]{:S(2)}) collective-permute-start(bf16[4,6,48,128]{3,2,1,0:T(8,128)(2,1)S(1)} %bitcast.26), channel_id=1, source_target_pairs={{0,1},{1,2},{2,3},{4,5},{5,6},{6,7},{8,9},{9,10},{10,11},{12,13},{... | collective-permute-start | bytes 884744 | tf_op jit(solution)/shard_map/ppermute | solution.py:128
  5.3 1.3 %collective-permute-start.2 = (bf16[4,6,48,128]{3,2,1,0:T(8,128)(2,1)S(1)}, bf16[4,6,48,128]{3,2,1,0:T(8,128)(2,1)S(1)}, u32[]{:S(2)}, u32[]{:S(2)}) collective-permute-start(bf16[4,6,48,128]{3,2,1,0:T(8,128)(2,1)S(1)} %bitcast.27), channel_id=1, source_target_pairs={{1,0},{2,1},{3,2},{5,4},{6,5},{7,6},{9,8},{10,9},{11,10},{13,12},{... | collective-permute-start | bytes 884744 | tf_op jit(solution)/shard_map/ppermute | solution.py:129
  6.6 1.2 slice_bitcast_fusion
  7.8 0.1 copy.10
  7.9 1.3 %collective-permute-start.7 = (bf16[4,6,48,128]{3,2,1,0:T(8,128)(2,1)S(1)}, bf16[4,6,48,128]{3,2,1,0:T(8,128)(2,1)S(1)}, u32[]{:S(2)}, u32[]{:S(2)}) collective-permute-start(bf16[4,6,48,128]{3,2,1,0:T(8,128)(2,1)S(1)} %bitcast.23), channel_id=1, source_target_pairs={{1,0},{2,1},{3,2},{5,4},{6,5},{7,6},{9,8},{10,9},{11,10},{13,12},{... | collective-permute-start | bytes 884744 | tf_op jit(solution)/shard_map/ppermute | solution.py:129
  9.2 4.6 %collective-permute-start.6 = (bf16[4,6,48,128]{3,2,1,0:T(8,128)(2,1)S(1)}, bf16[4,6,48,128]{3,2,1,0:T(8,128)(2,1)S(1)}, u32[]{:S(2)}, u32[]{:S(2)}) collective-permute-start(bf16[4,6,48,128]{3,2,1,0:T(8,128)(2,1)S(1)} %bitcast.24), channel_id=1, source_target_pairs={{0,1},{1,2},{2,3},{4,5},{5,6},{6,7},{8,9},{9,10},{10,11},{12,13},{... | collective-permute-start | bytes 884744 | tf_op jit(solution)/shard_map/ppermute | solution.py:128
  13.8 0.0 collective-permute-done.refs_1_
  13.8 0.7 collective-permute-start.1
  14.5 0.0 collective-permute-done.2.refs_6_
  14.5 1.3 %collective-permute-start.3 = (bf16[4,6,48,128]{3,2,1,0:T(8,128)(2,1)S(1)}, bf16[4,6,48,128]{3,2,1,0:T(8,128)(2,1)S(1)}, u32[]{:S(2)}, u32[]{:S(2)}) collective-permute-start(bf16[4,6,48,128]{3,2,1,0:T(8,128)(2,1)S(1)} %collective-permute-done.2.refs_6_), channel_id=1, source_target_pairs={{1,0},{2,1},{5,4},{6,5},{9,8},{10,9},{13,12},{14,13},{17,16},{18,1... | collective-permute-start | bytes 884744 | tf_op jit(solution)/shard_map/ppermute | solution.py:129
  15.8 0.1 collective-permute-done.7.refs_7_
  16.0 1.3 %collective-permute-start.8 = (bf16[4,6,48,128]{3,2,1,0:T(8,128)(2,1)S(1)}, bf16[4,6,48,128]{3,2,1,0:T(8,128)(2,1)S(1)}, u32[]{:S(2)}, u32[]{:S(2)}) collective-permute-start(bf16[4,6,48,128]{3,2,1,0:T(8,128)(2,1)S(1)} %collective-permute-done.7.refs_7_), channel_id=1, source_target_pairs={{1,0},{2,1},{5,4},{6,5},{9,8},{10,9},{13,12},{14,13},{17,16},{18,1... | collective-permute-start | bytes 884744 | tf_op jit(solution)/shard_map/ppermute | solution.py:129
  17.3 2.8 %collective-permute-done.6.refs_2_ = bf16[4,6,48,128]{3,2,1,0:T(8,128)(2,1)S(1)} collective-permute-done((bf16[4,6,48,128]{3,2,1,0:T(8,128)(2,1)S(1)}, bf16[4,6,48,128]{3,2,1,0:T(8,128)(2,1)S(1)}, u32[]{:S(2)}, u32[]{:S(2)}) %collective-permute-start.6) | collective-permute-done | bytes 294944 | tf_op jit(solution)/shard_map/ppermute | solution.py:128
  20.1 0.7 collective-permute-start.10
  20.8 0.0 collective-permute-done.1.refs_3_
  20.8 6.6 %collective-permute-done.3.refs_4_ = bf16[4,6,48,128]{3,2,1,0:T(8,128)(2,1)S(1)} collective-permute-done((bf16[4,6,48,128]{3,2,1,0:T(8,128)(2,1)S(1)}, bf16[4,6,48,128]{3,2,1,0:T(8,128)(2,1)S(1)}, u32[]{:S(2)}, u32[]{:S(2)}) %collective-permute-start.3) | collective-permute-done | bytes 294944 | tf_op jit(solution)/shard_map/ppermute | solution.py:129
  27.4 1.3 %collective-permute-start.4 = (bf16[4,6,48,128]{3,2,1,0:T(8,128)(2,1)S(1)}, bf16[4,6,48,128]{3,2,1,0:T(8,128)(2,1)}, u32[]{:S(2)}, u32[]{:S(2)}) collective-permute-start(bf16[4,6,48,128]{3,2,1,0:T(8,128)(2,1)S(1)} %collective-permute-done.3.refs_4_), channel_id=1, source_target_pairs={{1,0},{5,4},{9,8},{13,12},{17,16},{21,20},{25,24},{29,28},{33,32},... | collective-permute-start | bytes 884744 | tf_op jit(solution)/shard_map/ppermute | solution.py:129
  28.7 1.4 %collective-permute-start.5 = (bf16[4,6,48,128]{3,2,1,0:T(8,128)(2,1)S(1)}, bf16[4,6,48,128]{3,2,1,0:T(8,128)(2,1)}, u32[]{:S(2)}, u32[]{:S(2)}) collective-permute-start(bf16[4,6,48,128]{3,2,1,0:T(8,128)(2,1)S(1)} %collective-permute-done.1.refs_3_), channel_id=1, source_target_pairs={{2,3},{6,7},{10,11},{14,15},{18,19},{22,23},{26,27},{30,31},{34,35... | collective-permute-start | bytes 884744 | tf_op jit(solution)/shard_map/ppermute | solution.py:128
  30.1 2.4 %collective-permute-done.8.refs_5_ = bf16[4,6,48,128]{3,2,1,0:T(8,128)(2,1)S(1)} collective-permute-done((bf16[4,6,48,128]{3,2,1,0:T(8,128)(2,1)S(1)}, bf16[4,6,48,128]{3,2,1,0:T(8,128)(2,1)S(1)}, u32[]{:S(2)}, u32[]{:S(2)}) %collective-permute-start.8) | collective-permute-done | bytes 294944 | tf_op jit(solution)/shard_map/ppermute | solution.py:129
  32.4 1.3 %collective-permute-start.9 = (bf16[4,6,48,128]{3,2,1,0:T(8,128)(2,1)S(1)}, bf16[4,6,48,128]{3,2,1,0:T(8,128)(2,1)S(1)}, u32[]{:S(2)}, u32[]{:S(2)}) collective-permute-start(bf16[4,6,48,128]{3,2,1,0:T(8,128)(2,1)S(1)} %collective-permute-done.8.refs_5_), channel_id=1, source_target_pairs={{1,0},{5,4},{9,8},{13,12},{17,16},{21,20},{25,24},{29,28},{33,32},... | collective-permute-start | bytes 884744 | tf_op jit(solution)/shard_map/ppermute | solution.py:129
  33.7 0.0 collective-permute-done.10.refs_4_
  33.7 0.7 collective-permute-start.11
  34.4 0.0 copy-done
  34.5 0.7 constant_dynamic-slice_fusion.1
  35.3 2.8 %copy.9 = bf16[8,6,2,128,128]{4,3,2,1,0:T(8,128)(2,1)S(1)} copy(bf16[8,6,2,128,128]{4,2,1,3,0:T(2,128)(2,1)} %bitcast.33) | data formatting | bytes 6291456 | tf_op jit(solution)/shard_map/transpose | solution.py:160
  38.0 0.7 collective-permute-done.4.refs_2_
  38.8 0.0 collective-permute-done.5.refs_5_
  38.8 1.9 %forward.2 = (bf16[4,192,128]{2,1,0:T(8,128)(2,1)S(1)}, bf16[4,6,192,128]{3,2,1,0:T(8,128)(2,1)S(1)}) custom-call(bf16[4,6,48,128]{3,2,1,0:T(8,128)(2,1)S(1)} %bitcast.28, bf16[4,6,48,128]{3,2,1,0:T(8,128)(2,1)S(1)} %collective-permute-done.refs_1_, bf16[4,6,48,128]{3,2,1,0:T(8,128)(2,1)} %collective-permute-done.4.refs_2_, ...), custom_call_target="tpu_custom_call" | custom-call | flops 301989888 | bytes 2000000 | tf_op jit(solution)/shard_map/forward/pallas_call | solution.py:28
  40.7 4.5 %collective-permute-done.9.refs_3_ = bf16[4,6,48,128]{3,2,1,0:T(8,128)(2,1)S(1)} collective-permute-done((bf16[4,6,48,128]{3,2,1,0:T(8,128)(2,1)S(1)}, bf16[4,6,48,128]{3,2,1,0:T(8,128)(2,1)S(1)}, u32[]{:S(2)}, u32[]{:S(2)}) %collective-permute-start.9) | collective-permute-done | bytes 294944 | tf_op jit(solution)/shard_map/ppermute | solution.py:129
  45.2 0.0 collective-permute-done.11.refs_6_
  45.2 0.9 forward.3
  46.1 17.4 %all_to_all.24.parts_ref = bf16[16,96,128]{2,1,0:T(8,128)(2,1)S(1)} all-to-all(bf16[16,96,128]{2,1,0:T(8,128)(2,1)S(1)} %bitcast.29), channel_id=1, replica_groups=mesh['z_far'=6,'z_near'=2,'y_hi'=2,'x'=4,'core'=2,'event'=4] {'z_near','..., dimensions={0} | all-to-all | bytes 786432 | tf_op jit(solution)/shard_map/all_to_all | solution.py:19
  63.4 0.1 near_sum.1
  63.5 23.3 %all_to_all.25.parts_ref = bf16[6,96,128]{2,1,0:T(8,128)(2,1)S(1)} all-to-all(bf16[6,96,128]{2,1,0:T(8,128)(2,1)S(1)} %near_sum.1), channel_id=1, replica_groups=mesh['z_far'=6,'z_near'=2,'y_hi'=2,'x'=4,'core'=2,'event'=4] {'z_far'}, dimensions={0} | all-to-all | bytes 294912 | tf_op jit(solution)/shard_map/all_to_all | solution.py:19
  86.8 6.6 %collective-permute-start.12 = (bf16[96,128]{1,0:T(8,128)(2,1)S(1)}, bf16[96,128]{1,0:T(8,128)(2,1)S(1)}, u32[]{:S(2)}, u32[]{:S(2)}) collective-permute-start(bf16[96,128]{1,0:T(8,128)(2,1)S(1)} %get-tuple-element.43), channel_id=1, source_target_pairs={{0,32},{32,0},{1,33},{33,1},{2,34},{34,2},{3,35},{35,3},{4,36},{36... | collective-permute-start | bytes 73736 | tf_op jit(solution)/shard_map/ppermute | solution.py:191
  93.4 1.9 %collective-permute-done.12.other_ref = bf16[96,128]{1,0:T(8,128)(2,1)S(1)} collective-permute-done((bf16[96,128]{1,0:T(8,128)(2,1)S(1)}, bf16[96,128]{1,0:T(8,128)(2,1)S(1)}, u32[]{:S(2)}, u32[]{:S(2)}) %collective-permute-start.12) | collective-permute-done | bytes 24608 | tf_op jit(solution)/shard_map/ppermute | solution.py:191
  95.3 16.4 %all_to_all.26 = bf16[16,96,128]{2,1,0:T(8,128)(2,1)S(1)} all-to-all(bf16[16,96,128]{2,1,0:T(8,128)(2,1)S(1)} %resid.1), channel_id=1, replica_groups=mesh['z_far'=6,'z_near'=2,'y_hi'=2,'x'=4,'core'=2,'event'=4] {'z_near','..., dimensions={0} | all-to-all | bytes 786432 | tf_op jit(solution)/shard_map/all_to_all | solution.py:19
  111.8 2.1 %backward.1 = f32[4,32]{1,0:T(4,128)S(1)} custom-call(bf16[4,6,192,128]{3,2,1,0:T(8,128)(2,1)S(1)} %get-tuple-element.29.refs_0_, bf16[4,6,192,128]{3,2,1,0:T(8,128)(2,1)S(1)} %get-tuple-element.40.refs_1_, bf16[8,192,128]{2,1,0:T(8,128)(2,1)S(1)} %bitcast.22, bf16[8,6,256,128]{3,2,1,0:T(8,128)(2,1)S(1)} %bitcast.21), custom_call_target="tpu_custom_call" | custom-call | flops 603979776 | bytes 2000000 | tf_op jit(solution)/shard_map/backward/pallas_call | solution.py:28
  113.8 7.9 %all_to_all.27 = f32[4,1,32]{2,1,0:T(1,128)S(1)} all-to-all(f32[4,1,32]{2,1,0:T(1,128)S(1)} %bitcast.32), channel_id=1, replica_groups=mesh['z_far'=6,'z_near'=2,'y_hi'=2,'x'=4,'core'=2,'event'=4] {'event'}, dimensions={0} | all-to-all | bytes 1024 | tf_op jit(solution)/shard_map/all_to_all | solution.py:19
  121.8 0.5 broadcast_multiply_fusion
  (6 shorter events, 0.1 us)
Async XLA Ops:
  0.0 34.4 %copy-start = (f32[128]{0:T(128)S(1)}, f32[128]{0:T(128)}, u32[]{:S(2)}) copy-start(f32[128]{0:T(128)} %param.6) | copy-start | bytes 1540
  1.3 12.6 %collective-permute-start = (bf16[4,6,48,128]{3,2,1,0:T(8,128)(2,1)S(1)}, bf16[4,6,48,128]{3,2,1,0:T(8,128)(2,1)S(1)}, u32[]{:S(2)}, u32[]{:S(2)}) collective-permute-start(bf16[4,6,48,128]{3,2,1,0:T(8,128)(2,1)S(1)} %bitcast.26), channel_id=1, source_target_pairs={{0,1},{1,2},{2,3},{4,5},{5,6},{6,7},{8,9},{9,10},{10,11},{12,13},{... | collective-permute-start | bytes 884744 | tf_op jit(solution)/shard_map/ppermute | solution.py:128
  5.3 9.2 %collective-permute-start.2 = (bf16[4,6,48,128]{3,2,1,0:T(8,128)(2,1)S(1)}, bf16[4,6,48,128]{3,2,1,0:T(8,128)(2,1)S(1)}, u32[]{:S(2)}, u32[]{:S(2)}) collective-permute-start(bf16[4,6,48,128]{3,2,1,0:T(8,128)(2,1)S(1)} %bitcast.27), channel_id=1, source_target_pairs={{1,0},{2,1},{3,2},{5,4},{6,5},{7,6},{9,8},{10,9},{11,10},{13,12},{... | collective-permute-start | bytes 884744 | tf_op jit(solution)/shard_map/ppermute | solution.py:129
  7.9 8.1 %collective-permute-start.7 = (bf16[4,6,48,128]{3,2,1,0:T(8,128)(2,1)S(1)}, bf16[4,6,48,128]{3,2,1,0:T(8,128)(2,1)S(1)}, u32[]{:S(2)}, u32[]{:S(2)}) collective-permute-start(bf16[4,6,48,128]{3,2,1,0:T(8,128)(2,1)S(1)} %bitcast.23), channel_id=1, source_target_pairs={{1,0},{2,1},{3,2},{5,4},{6,5},{7,6},{9,8},{10,9},{11,10},{13,12},{... | collective-permute-start | bytes 884744 | tf_op jit(solution)/shard_map/ppermute | solution.py:129
  9.2 10.9 %collective-permute-start.6 = (bf16[4,6,48,128]{3,2,1,0:T(8,128)(2,1)S(1)}, bf16[4,6,48,128]{3,2,1,0:T(8,128)(2,1)S(1)}, u32[]{:S(2)}, u32[]{:S(2)}) collective-permute-start(bf16[4,6,48,128]{3,2,1,0:T(8,128)(2,1)S(1)} %bitcast.24), channel_id=1, source_target_pairs={{0,1},{1,2},{2,3},{4,5},{5,6},{6,7},{8,9},{9,10},{10,11},{12,13},{... | collective-permute-start | bytes 884744 | tf_op jit(solution)/shard_map/ppermute | solution.py:128
  13.8 6.9 %collective-permute-start.1 = (bf16[4,6,48,128]{3,2,1,0:T(8,128)(2,1)S(1)}, bf16[4,6,48,128]{3,2,1,0:T(8,128)(2,1)S(1)}, u32[]{:S(2)}, u32[]{:S(2)}) collective-permute-start(bf16[4,6,48,128]{3,2,1,0:T(8,128)(2,1)S(1)} %collective-permute-done.refs_1_), channel_id=1, source_target_pairs={{1,2},{2,3},{5,6},{6,7},{9,10},{10,11},{13,14},{14,15},{17,18},{18... | collective-permute-start | bytes 884744 | tf_op jit(solution)/shard_map/ppermute | solution.py:128
  14.5 12.8 %collective-permute-start.3 = (bf16[4,6,48,128]{3,2,1,0:T(8,128)(2,1)S(1)}, bf16[4,6,48,128]{3,2,1,0:T(8,128)(2,1)S(1)}, u32[]{:S(2)}, u32[]{:S(2)}) collective-permute-start(bf16[4,6,48,128]{3,2,1,0:T(8,128)(2,1)S(1)} %collective-permute-done.2.refs_6_), channel_id=1, source_target_pairs={{1,0},{2,1},{5,4},{6,5},{9,8},{10,9},{13,12},{14,13},{17,16},{18,1... | collective-permute-start | bytes 884744 | tf_op jit(solution)/shard_map/ppermute | solution.py:129
  16.0 16.4 %collective-permute-start.8 = (bf16[4,6,48,128]{3,2,1,0:T(8,128)(2,1)S(1)}, bf16[4,6,48,128]{3,2,1,0:T(8,128)(2,1)S(1)}, u32[]{:S(2)}, u32[]{:S(2)}) collective-permute-start(bf16[4,6,48,128]{3,2,1,0:T(8,128)(2,1)S(1)} %collective-permute-done.7.refs_7_), channel_id=1, source_target_pairs={{1,0},{2,1},{5,4},{6,5},{9,8},{10,9},{13,12},{14,13},{17,16},{18,1... | collective-permute-start | bytes 884744 | tf_op jit(solution)/shard_map/ppermute | solution.py:129
  20.1 13.6 %collective-permute-start.10 = (bf16[4,6,48,128]{3,2,1,0:T(8,128)(2,1)S(1)}, bf16[4,6,48,128]{3,2,1,0:T(8,128)(2,1)S(1)}, u32[]{:S(2)}, u32[]{:S(2)}) collective-permute-start(bf16[4,6,48,128]{3,2,1,0:T(8,128)(2,1)S(1)} %collective-permute-done.6.refs_2_), channel_id=1, source_target_pairs={{1,2},{2,3},{5,6},{6,7},{9,10},{10,11},{13,14},{14,15},{17,18},{18... | collective-permute-start | bytes 884744 | tf_op jit(solution)/shard_map/ppermute | solution.py:128
  27.4 11.4 %collective-permute-start.4 = (bf16[4,6,48,128]{3,2,1,0:T(8,128)(2,1)S(1)}, bf16[4,6,48,128]{3,2,1,0:T(8,128)(2,1)}, u32[]{:S(2)}, u32[]{:S(2)}) collective-permute-start(bf16[4,6,48,128]{3,2,1,0:T(8,128)(2,1)S(1)} %collective-permute-done.3.refs_4_), channel_id=1, source_target_pairs={{1,0},{5,4},{9,8},{13,12},{17,16},{21,20},{25,24},{29,28},{33,32},... | collective-permute-start | bytes 884744 | tf_op jit(solution)/shard_map/ppermute | solution.py:129
  28.7 10.1 %collective-permute-start.5 = (bf16[4,6,48,128]{3,2,1,0:T(8,128)(2,1)S(1)}, bf16[4,6,48,128]{3,2,1,0:T(8,128)(2,1)}, u32[]{:S(2)}, u32[]{:S(2)}) collective-permute-start(bf16[4,6,48,128]{3,2,1,0:T(8,128)(2,1)S(1)} %collective-permute-done.1.refs_3_), channel_id=1, source_target_pairs={{2,3},{6,7},{10,11},{14,15},{18,19},{22,23},{26,27},{30,31},{34,35... | collective-permute-start | bytes 884744 | tf_op jit(solution)/shard_map/ppermute | solution.py:128
  32.4 12.7 %collective-permute-start.9 = (bf16[4,6,48,128]{3,2,1,0:T(8,128)(2,1)S(1)}, bf16[4,6,48,128]{3,2,1,0:T(8,128)(2,1)S(1)}, u32[]{:S(2)}, u32[]{:S(2)}) collective-permute-start(bf16[4,6,48,128]{3,2,1,0:T(8,128)(2,1)S(1)} %collective-permute-done.8.refs_5_), channel_id=1, source_target_pairs={{1,0},{5,4},{9,8},{13,12},{17,16},{21,20},{25,24},{29,28},{33,32},... | collective-permute-start | bytes 884744 | tf_op jit(solution)/shard_map/ppermute | solution.py:129
  33.7 11.4 %collective-permute-start.11 = (bf16[4,6,48,128]{3,2,1,0:T(8,128)(2,1)S(1)}, bf16[4,6,48,128]{3,2,1,0:T(8,128)(2,1)S(1)}, u32[]{:S(2)}, u32[]{:S(2)}) collective-permute-start(bf16[4,6,48,128]{3,2,1,0:T(8,128)(2,1)S(1)} %collective-permute-done.10.refs_4_), channel_id=1, source_target_pairs={{2,3},{6,7},{10,11},{14,15},{18,19},{22,23},{26,27},{30,31},{34,35... | collective-permute-start | bytes 884744 | tf_op jit(solution)/shard_map/ppermute | solution.py:128
  86.8 8.5 %collective-permute-start.12 = (bf16[96,128]{1,0:T(8,128)(2,1)S(1)}, bf16[96,128]{1,0:T(8,128)(2,1)S(1)}, u32[]{:S(2)}, u32[]{:S(2)}) collective-permute-start(bf16[96,128]{1,0:T(8,128)(2,1)S(1)} %get-tuple-element.43), channel_id=1, source_target_pairs={{0,32},{32,0},{1,33},{33,1},{2,34},{34,2},{3,35},{35,3},{4,36},{36... | collective-permute-start | bytes 73736 | tf_op jit(solution)/shard_map/ppermute | solution.py:191

commit v5 on v3

--- a/solution.py
+++ b/solution.py
@@ -64,7 +64,7 @@
         out_ref[start + i] = jnp.concatenate(rows, 0).astype(out_ref.dtype)
         return carry
 
-    lax.fori_loop(0, freqs, step, 0, unroll=2)
+    lax.fori_loop(0, freqs, step, 0, unroll=4)
 
 
 def near_sum_kernel(parts_ref, out_ref):
@@ -115,7 +115,7 @@
                     acc = acc + terms[j:j + 8]
             return acc
 
-        acc = lax.fori_loop(0, freqs, step, acc, unroll=2)
+        acc = lax.fori_loop(0, freqs, step, acc, unroll=4)
     acc = acc.sum(0, keepdims=True)
     parts, width = out_ref.shape
     for j in range(parts):

time: 123 us -> 123 us (level)
  transfers between devices with their start and end apart: 13 -> 13, of which waited for: 7 -> 7; matrix products, arithmetic and copies ran while one was open for 4% -> 4% of each run, Pallas kernels for 2% -> 1%
where the time goes in v5:
time: 123 us; the launch traced here: 122 us
  blocking collectives  65 us (53%)
  starting transfers between devices  26.4 us (21%)
  waiting for transfers between devices  19.6 us (16%)
  local copies, waits for them, and re-layouts  6.01 us (5%)
  Pallas kernels  4.03 us (3%)
    all_to_all x4, blocking collectives, exchange(): return lax.all_to_all(parts, axes, 0, 0, tiled=True)  65 us
    ppermute x6, waiting for transfers between devices, hop(): lax.ppermute(down, 'event', [(i, i - 1) for i in range(1, n + 1 - k)])  14.6 us
    ppermute x6, starting transfers between devices, hop(): lax.ppermute(up, 'event', [(i, i + 1) for i in range(k - 1, n - 1)])  12.1 us
    ppermute x6, starting transfers between devices, hop(): lax.ppermute(down, 'event', [(i, i - 1) for i in range(1, n + 1 - k)])  7.72 us
    ppermute x1, starting transfers between devices, body(): other = lax.ppermute(summed, 'y_hi', [(0, 1), (1, 0)])  6.56 us
    pallas_call x6, Pallas kernels, call(): pl.pallas_call(kernel, in_specs=[WHOLE] * len(args), out_specs=WHOLE if s...  4.03 us
    ppermute x6, waiting for transfers between devices, hop(): lax.ppermute(up, 'event', [(i, i + 1) for i in range(k - 1, n - 1)])  2.81 us
    transpose x1, local copies, waits for them, and re-layouts, body(): green.transpose(0, 3, 2, 1, 4).reshape(freqs, comps, 2 * recv, cells)  2.76 us
  transfers between devices with their start and end apart: 13, of which 7 were waited for; matrix products, arithmetic and copies ran while one was open for 4% of the time, Pallas kernels for 1%

profile of v5, /device:TPU:1, one launch (start us, length us, event | category | flops | bytes accessed | tf_op | source)
XLA Modules:
  0.0 121.8 jit_solution(10174538281665197680)
XLA Ops:
  0.0 0.0 copy-start
  0.0 1.2 slice_bitcast_fusion.1
  1.2 0.1 copy.8
  1.3 4.0 %collective-permute-start = (bf16[4,6,48,128]{3,2,1,0:T(8,128)(2,1)S(1)}, bf16[4,6,48,128]{3,2,1,0:T(8,128)(2,1)S(1)}, u32[]{:S(2)}, u32[]{:S(2)}) collective-permute-start(bf16[4,6,48,128]{3,2,1,0:T(8,128)(2,1)S(1)} %bitcast.26), channel_id=1, source_target_pairs={{0,1},{1,2},{2,3},{4,5},{5,6},{6,7},{8,9},{9,10},{10,11},{12,13},{... | collective-permute-start | bytes 884744 | tf_op jit(solution)/shard_map/ppermute | solution.py:127
  5.3 1.3 %collective-permute-start.2 = (bf16[4,6,48,128]{3,2,1,0:T(8,128)(2,1)S(1)}, bf16[4,6,48,128]{3,2,1,0:T(8,128)(2,1)S(1)}, u32[]{:S(2)}, u32[]{:S(2)}) collective-permute-start(bf16[4,6,48,128]{3,2,1,0:T(8,128)(2,1)S(1)} %bitcast.27), channel_id=1, source_target_pairs={{1,0},{2,1},{3,2},{5,4},{6,5},{7,6},{9,8},{10,9},{11,10},{13,12},{... | collective-permute-start | bytes 884744 | tf_op jit(solution)/shard_map/ppermute | solution.py:128
  6.6 1.2 slice_bitcast_fusion
  7.8 0.1 copy.10
  7.9 1.3 %collective-permute-start.7 = (bf16[4,6,48,128]{3,2,1,0:T(8,128)(2,1)S(1)}, bf16[4,6,48,128]{3,2,1,0:T(8,128)(2,1)S(1)}, u32[]{:S(2)}, u32[]{:S(2)}) collective-permute-start(bf16[4,6,48,128]{3,2,1,0:T(8,128)(2,1)S(1)} %bitcast.23), channel_id=1, source_target_pairs={{1,0},{2,1},{3,2},{5,4},{6,5},{7,6},{9,8},{10,9},{11,10},{13,12},{... | collective-permute-start | bytes 884744 | tf_op jit(solution)/shard_map/ppermute | solution.py:128
  9.2 4.6 %collective-permute-start.6 = (bf16[4,6,48,128]{3,2,1,0:T(8,128)(2,1)S(1)}, bf16[4,6,48,128]{3,2,1,0:T(8,128)(2,1)S(1)}, u32[]{:S(2)}, u32[]{:S(2)}) collective-permute-start(bf16[4,6,48,128]{3,2,1,0:T(8,128)(2,1)S(1)} %bitcast.24), channel_id=1, source_target_pairs={{0,1},{1,2},{2,3},{4,5},{5,6},{6,7},{8,9},{9,10},{10,11},{12,13},{... | collective-permute-start | bytes 884744 | tf_op jit(solution)/shard_map/ppermute | solution.py:127
  13.8 0.0 collective-permute-done.refs_1_
  13.8 0.7 collective-permute-start.1
  14.5 0.0 collective-permute-done.2.refs_6_
  14.5 1.3 %collective-permute-start.3 = (bf16[4,6,48,128]{3,2,1,0:T(8,128)(2,1)S(1)}, bf16[4,6,48,128]{3,2,1,0:T(8,128)(2,1)S(1)}, u32[]{:S(2)}, u32[]{:S(2)}) collective-permute-start(bf16[4,6,48,128]{3,2,1,0:T(8,128)(2,1)S(1)} %collective-permute-done.2.refs_6_), channel_id=1, source_target_pairs={{1,0},{2,1},{5,4},{6,5},{9,8},{10,9},{13,12},{14,13},{17,16},{18,1... | collective-permute-start | bytes 884744 | tf_op jit(solution)/shard_map/ppermute | solution.py:128
  15.8 0.1 collective-permute-done.7.refs_7_
  16.0 1.3 %collective-permute-start.8 = (bf16[4,6,48,128]{3,2,1,0:T(8,128)(2,1)S(1)}, bf16[4,6,48,128]{3,2,1,0:T(8,128)(2,1)S(1)}, u32[]{:S(2)}, u32[]{:S(2)}) collective-permute-start(bf16[4,6,48,128]{3,2,1,0:T(8,128)(2,1)S(1)} %collective-permute-done.7.refs_7_), channel_id=1, source_target_pairs={{1,0},{2,1},{5,4},{6,5},{9,8},{10,9},{13,12},{14,13},{17,16},{18,1... | collective-permute-start | bytes 884744 | tf_op jit(solution)/shard_map/ppermute | solution.py:128
  17.3 2.8 %collective-permute-done.6.refs_2_ = bf16[4,6,48,128]{3,2,1,0:T(8,128)(2,1)S(1)} collective-permute-done((bf16[4,6,48,128]{3,2,1,0:T(8,128)(2,1)S(1)}, bf16[4,6,48,128]{3,2,1,0:T(8,128)(2,1)S(1)}, u32[]{:S(2)}, u32[]{:S(2)}) %collective-permute-start.6) | collective-permute-done | bytes 294944 | tf_op jit(solution)/shard_map/ppermute | solution.py:127
  20.1 0.7 collective-permute-start.10
  20.8 0.0 collective-permute-done.1.refs_3_
  20.8 6.6 %collective-permute-done.3.refs_4_ = bf16[4,6,48,128]{3,2,1,0:T(8,128)(2,1)S(1)} collective-permute-done((bf16[4,6,48,128]{3,2,1,0:T(8,128)(2,1)S(1)}, bf16[4,6,48,128]{3,2,1,0:T(8,128)(2,1)S(1)}, u32[]{:S(2)}, u32[]{:S(2)}) %collective-permute-start.3) | collective-permute-done | bytes 294944 | tf_op jit(solution)/shard_map/ppermute | solution.py:128
  27.4 1.3 %collective-permute-start.4 = (bf16[4,6,48,128]{3,2,1,0:T(8,128)(2,1)S(1)}, bf16[4,6,48,128]{3,2,1,0:T(8,128)(2,1)}, u32[]{:S(2)}, u32[]{:S(2)}) collective-permute-start(bf16[4,6,48,128]{3,2,1,0:T(8,128)(2,1)S(1)} %collective-permute-done.3.refs_4_), channel_id=1, source_target_pairs={{1,0},{5,4},{9,8},{13,12},{17,16},{21,20},{25,24},{29,28},{33,32},... | collective-permute-start | bytes 884744 | tf_op jit(solution)/shard_map/ppermute | solution.py:128
  28.7 1.4 %collective-permute-start.5 = (bf16[4,6,48,128]{3,2,1,0:T(8,128)(2,1)S(1)}, bf16[4,6,48,128]{3,2,1,0:T(8,128)(2,1)}, u32[]{:S(2)}, u32[]{:S(2)}) collective-permute-start(bf16[4,6,48,128]{3,2,1,0:T(8,128)(2,1)S(1)} %collective-permute-done.1.refs_3_), channel_id=1, source_target_pairs={{2,3},{6,7},{10,11},{14,15},{18,19},{22,23},{26,27},{30,31},{34,35... | collective-permute-start | bytes 884744 | tf_op jit(solution)/shard_map/ppermute | solution.py:127
  30.1 2.4 %collective-permute-done.8.refs_5_ = bf16[4,6,48,128]{3,2,1,0:T(8,128)(2,1)S(1)} collective-permute-done((bf16[4,6,48,128]{3,2,1,0:T(8,128)(2,1)S(1)}, bf16[4,6,48,128]{3,2,1,0:T(8,128)(2,1)S(1)}, u32[]{:S(2)}, u32[]{:S(2)}) %collective-permute-start.8) | collective-permute-done | bytes 294944 | tf_op jit(solution)/shard_map/ppermute | solution.py:128
  32.4 1.3 %collective-permute-start.9 = (bf16[4,6,48,128]{3,2,1,0:T(8,128)(2,1)S(1)}, bf16[4,6,48,128]{3,2,1,0:T(8,128)(2,1)S(1)}, u32[]{:S(2)}, u32[]{:S(2)}) collective-permute-start(bf16[4,6,48,128]{3,2,1,0:T(8,128)(2,1)S(1)} %collective-permute-done.8.refs_5_), channel_id=1, source_target_pairs={{1,0},{5,4},{9,8},{13,12},{17,16},{21,20},{25,24},{29,28},{33,32},... | collective-permute-start | bytes 884744 | tf_op jit(solution)/shard_map/ppermute | solution.py:128
  33.7 0.0 collective-permute-done.10.refs_4_
  33.7 0.7 collective-permute-start.11
  34.4 0.0 copy-done
  34.5 0.7 constant_dynamic-slice_fusion.1
  35.3 2.8 %copy.9 = bf16[8,6,2,128,128]{4,3,2,1,0:T(8,128)(2,1)S(1)} copy(bf16[8,6,2,128,128]{4,2,1,3,0:T(2,128)(2,1)} %bitcast.33) | data formatting | bytes 6291456 | tf_op jit(solution)/shard_map/transpose | solution.py:159
  38.0 0.7 collective-permute-done.4.refs_2_
  38.8 0.0 collective-permute-done.5.refs_5_
  38.8 1.7 %forward.2 = (bf16[4,192,128]{2,1,0:T(8,128)(2,1)S(1)}, bf16[4,6,192,128]{3,2,1,0:T(8,128)(2,1)S(1)}) custom-call(bf16[4,6,48,128]{3,2,1,0:T(8,128)(2,1)S(1)} %bitcast.28, bf16[4,6,48,128]{3,2,1,0:T(8,128)(2,1)S(1)} %collective-permute-done.refs_1_, bf16[4,6,48,128]{3,2,1,0:T(8,128)(2,1)} %collective-permute-done.4.refs_2_, ...), custom_call_target="tpu_custom_call" | custom-call | flops 301989888 | bytes 2000000 | tf_op jit(solution)/shard_map/forward/pallas_call | solution.py:28
  40.5 4.7 %collective-permute-done.9.refs_3_ = bf16[4,6,48,128]{3,2,1,0:T(8,128)(2,1)S(1)} collective-permute-done((bf16[4,6,48,128]{3,2,1,0:T(8,128)(2,1)S(1)}, bf16[4,6,48,128]{3,2,1,0:T(8,128)(2,1)S(1)}, u32[]{:S(2)}, u32[]{:S(2)}) %collective-permute-start.9) | collective-permute-done | bytes 294944 | tf_op jit(solution)/shard_map/ppermute | solution.py:128
  45.2 0.0 collective-permute-done.11.refs_6_
  45.2 0.7 forward.3
  45.9 17.4 %all_to_all.24.parts_ref = bf16[16,96,128]{2,1,0:T(8,128)(2,1)S(1)} all-to-all(bf16[16,96,128]{2,1,0:T(8,128)(2,1)S(1)} %bitcast.29), channel_id=1, replica_groups=mesh['z_far'=6,'z_near'=2,'y_hi'=2,'x'=4,'core'=2,'event'=4] {'z_near','..., dimensions={0} | all-to-all | bytes 786432 | tf_op jit(solution)/shard_map/all_to_all | solution.py:19
  63.2 0.1 near_sum.1
  63.3 23.3 %all_to_all.25.parts_ref = bf16[6,96,128]{2,1,0:T(8,128)(2,1)S(1)} all-to-all(bf16[6,96,128]{2,1,0:T(8,128)(2,1)S(1)} %near_sum.1), channel_id=1, replica_groups=mesh['z_far'=6,'z_near'=2,'y_hi'=2,'x'=4,'core'=2,'event'=4] {'z_far'}, dimensions={0} | all-to-all | bytes 294912 | tf_op jit(solution)/shard_map/all_to_all | solution.py:19
  86.6 6.6 %collective-permute-start.12 = (f32[96,128]{1,0:T(8,128)S(1)}, f32[96,128]{1,0:T(8,128)S(1)}, u32[]{:S(2)}, u32[]{:S(2)}) collective-permute-start(f32[96,128]{1,0:T(8,128)S(1)} %far_sum.1.mine_ref), channel_id=1, source_target_pairs={{0,32},{32,0},{1,33},{33,1},{2,34},{34,2},{3,35},{35,3},{4,36},{36... | collective-permute-start | bytes 147464 | tf_op jit(solution)/shard_map/ppermute | solution.py:189
  93.2 2.2 %collective-permute-done.12.other_ref = f32[96,128]{1,0:T(8,128)S(1)} collective-permute-done((f32[96,128]{1,0:T(8,128)S(1)}, f32[96,128]{1,0:T(8,128)S(1)}, u32[]{:S(2)}, u32[]{:S(2)}) %collective-permute-start.12) | collective-permute-done | bytes 49184 | tf_op jit(solution)/shard_map/ppermute | solution.py:189
  95.4 16.4 %all_to_all.26 = bf16[16,96,128]{2,1,0:T(8,128)(2,1)S(1)} all-to-all(bf16[16,96,128]{2,1,0:T(8,128)(2,1)S(1)} %resid.1), channel_id=1, replica_groups=mesh['z_far'=6,'z_near'=2,'y_hi'=2,'x'=4,'core'=2,'event'=4] {'z_near','..., dimensions={0} | all-to-all | bytes 786432 | tf_op jit(solution)/shard_map/all_to_all | solution.py:19
  111.8 1.5 %backward.1 = f32[4,32]{1,0:T(4,128)S(1)} custom-call(bf16[4,6,192,128]{3,2,1,0:T(8,128)(2,1)S(1)} %get-tuple-element.27.refs_0_, bf16[4,6,192,128]{3,2,1,0:T(8,128)(2,1)S(1)} %get-tuple-element.38.refs_1_, bf16[8,192,128]{2,1,0:T(8,128)(2,1)S(1)} %bitcast.22, bf16[8,6,256,128]{3,2,1,0:T(8,128)(2,1)S(1)} %bitcast.21), custom_call_target="tpu_custom_call" | custom-call | flops 603979776 | bytes 2000000 | tf_op jit(solution)/shard_map/backward/pallas_call | solution.py:28
  113.4 7.9 %all_to_all.27 = f32[4,1,32]{2,1,0:T(1,128)S(1)} all-to-all(f32[4,1,32]{2,1,0:T(1,128)S(1)} %bitcast.32), channel_id=1, replica_groups=mesh['z_far'=6,'z_near'=2,'y_hi'=2,'x'=4,'core'=2,'event'=4] {'event'}, dimensions={0} | all-to-all | bytes 1024 | tf_op jit(solution)/shard_map/all_to_all | solution.py:19
  121.3 0.5 broadcast_multiply_fusion
  (6 shorter events, 0.1 us)
Async XLA Ops:
  0.0 34.4 %copy-start = (f32[128]{0:T(128)S(1)}, f32[128]{0:T(128)}, u32[]{:S(2)}) copy-start(f32[128]{0:T(128)} %param.6) | copy-start | bytes 1540
  1.3 12.6 %collective-permute-start = (bf16[4,6,48,128]{3,2,1,0:T(8,128)(2,1)S(1)}, bf16[4,6,48,128]{3,2,1,0:T(8,128)(2,1)S(1)}, u32[]{:S(2)}, u32[]{:S(2)}) collective-permute-start(bf16[4,6,48,128]{3,2,1,0:T(8,128)(2,1)S(1)} %bitcast.26), channel_id=1, source_target_pairs={{0,1},{1,2},{2,3},{4,5},{5,6},{6,7},{8,9},{9,10},{10,11},{12,13},{... | collective-permute-start | bytes 884744 | tf_op jit(solution)/shard_map/ppermute | solution.py:127
  5.3 9.2 %collective-permute-start.2 = (bf16[4,6,48,128]{3,2,1,0:T(8,128)(2,1)S(1)}, bf16[4,6,48,128]{3,2,1,0:T(8,128)(2,1)S(1)}, u32[]{:S(2)}, u32[]{:S(2)}) collective-permute-start(bf16[4,6,48,128]{3,2,1,0:T(8,128)(2,1)S(1)} %bitcast.27), channel_id=1, source_target_pairs={{1,0},{2,1},{3,2},{5,4},{6,5},{7,6},{9,8},{10,9},{11,10},{13,12},{... | collective-permute-start | bytes 884744 | tf_op jit(solution)/shard_map/ppermute | solution.py:128
  7.9 8.1 %collective-permute-start.7 = (bf16[4,6,48,128]{3,2,1,0:T(8,128)(2,1)S(1)}, bf16[4,6,48,128]{3,2,1,0:T(8,128)(2,1)S(1)}, u32[]{:S(2)}, u32[]{:S(2)}) collective-permute-start(bf16[4,6,48,128]{3,2,1,0:T(8,128)(2,1)S(1)} %bitcast.23), channel_id=1, source_target_pairs={{1,0},{2,1},{3,2},{5,4},{6,5},{7,6},{9,8},{10,9},{11,10},{13,12},{... | collective-permute-start | bytes 884744 | tf_op jit(solution)/shard_map/ppermute | solution.py:128
  9.2 10.9 %collective-permute-start.6 = (bf16[4,6,48,128]{3,2,1,0:T(8,128)(2,1)S(1)}, bf16[4,6,48,128]{3,2,1,0:T(8,128)(2,1)S(1)}, u32[]{:S(2)}, u32[]{:S(2)}) collective-permute-start(bf16[4,6,48,128]{3,2,1,0:T(8,128)(2,1)S(1)} %bitcast.24), channel_id=1, source_target_pairs={{0,1},{1,2},{2,3},{4,5},{5,6},{6,7},{8,9},{9,10},{10,11},{12,13},{... | collective-permute-start | bytes 884744 | tf_op jit(solution)/shard_map/ppermute | solution.py:127
  13.8 6.9 %collective-permute-start.1 = (bf16[4,6,48,128]{3,2,1,0:T(8,128)(2,1)S(1)}, bf16[4,6,48,128]{3,2,1,0:T(8,128)(2,1)S(1)}, u32[]{:S(2)}, u32[]{:S(2)}) collective-permute-start(bf16[4,6,48,128]{3,2,1,0:T(8,128)(2,1)S(1)} %collective-permute-done.refs_1_), channel_id=1, source_target_pairs={{1,2},{2,3},{5,6},{6,7},{9,10},{10,11},{13,14},{14,15},{17,18},{18... | collective-permute-start | bytes 884744 | tf_op jit(solution)/shard_map/ppermute | solution.py:127
  14.5 12.8 %collective-permute-start.3 = (bf16[4,6,48,128]{3,2,1,0:T(8,128)(2,1)S(1)}, bf16[4,6,48,128]{3,2,1,0:T(8,128)(2,1)S(1)}, u32[]{:S(2)}, u32[]{:S(2)}) collective-permute-start(bf16[4,6,48,128]{3,2,1,0:T(8,128)(2,1)S(1)} %collective-permute-done.2.refs_6_), channel_id=1, source_target_pairs={{1,0},{2,1},{5,4},{6,5},{9,8},{10,9},{13,12},{14,13},{17,16},{18,1... | collective-permute-start | bytes 884744 | tf_op jit(solution)/shard_map/ppermute | solution.py:128
  16.0 16.4 %collective-permute-start.8 = (bf16[4,6,48,128]{3,2,1,0:T(8,128)(2,1)S(1)}, bf16[4,6,48,128]{3,2,1,0:T(8,128)(2,1)S(1)}, u32[]{:S(2)}, u32[]{:S(2)}) collective-permute-start(bf16[4,6,48,128]{3,2,1,0:T(8,128)(2,1)S(1)} %collective-permute-done.7.refs_7_), channel_id=1, source_target_pairs={{1,0},{2,1},{5,4},{6,5},{9,8},{10,9},{13,12},{14,13},{17,16},{18,1... | collective-permute-start | bytes 884744 | tf_op jit(solution)/shard_map/ppermute | solution.py:128
  20.1 13.6 %collective-permute-start.10 = (bf16[4,6,48,128]{3,2,1,0:T(8,128)(2,1)S(1)}, bf16[4,6,48,128]{3,2,1,0:T(8,128)(2,1)S(1)}, u32[]{:S(2)}, u32[]{:S(2)}) collective-permute-start(bf16[4,6,48,128]{3,2,1,0:T(8,128)(2,1)S(1)} %collective-permute-done.6.refs_2_), channel_id=1, source_target_pairs={{1,2},{2,3},{5,6},{6,7},{9,10},{10,11},{13,14},{14,15},{17,18},{18... | collective-permute-start | bytes 884744 | tf_op jit(solution)/shard_map/ppermute | solution.py:127
  27.4 11.4 %collective-permute-start.4 = (bf16[4,6,48,128]{3,2,1,0:T(8,128)(2,1)S(1)}, bf16[4,6,48,128]{3,2,1,0:T(8,128)(2,1)}, u32[]{:S(2)}, u32[]{:S(2)}) collective-permute-start(bf16[4,6,48,128]{3,2,1,0:T(8,128)(2,1)S(1)} %collective-permute-done.3.refs_4_), channel_id=1, source_target_pairs={{1,0},{5,4},{9,8},{13,12},{17,16},{21,20},{25,24},{29,28},{33,32},... | collective-permute-start | bytes 884744 | tf_op jit(solution)/shard_map/ppermute | solution.py:128
  28.7 10.1 %collective-permute-start.5 = (bf16[4,6,48,128]{3,2,1,0:T(8,128)(2,1)S(1)}, bf16[4,6,48,128]{3,2,1,0:T(8,128)(2,1)}, u32[]{:S(2)}, u32[]{:S(2)}) collective-permute-start(bf16[4,6,48,128]{3,2,1,0:T(8,128)(2,1)S(1)} %collective-permute-done.1.refs_3_), channel_id=1, source_target_pairs={{2,3},{6,7},{10,11},{14,15},{18,19},{22,23},{26,27},{30,31},{34,35... | collective-permute-start | bytes 884744 | tf_op jit(solution)/shard_map/ppermute | solution.py:127
  32.4 12.7 %collective-permute-start.9 = (bf16[4,6,48,128]{3,2,1,0:T(8,128)(2,1)S(1)}, bf16[4,6,48,128]{3,2,1,0:T(8,128)(2,1)S(1)}, u32[]{:S(2)}, u32[]{:S(2)}) collective-permute-start(bf16[4,6,48,128]{3,2,1,0:T(8,128)(2,1)S(1)} %collective-permute-done.8.refs_5_), channel_id=1, source_target_pairs={{1,0},{5,4},{9,8},{13,12},{17,16},{21,20},{25,24},{29,28},{33,32},... | collective-permute-start | bytes 884744 | tf_op jit(solution)/shard_map/ppermute | solution.py:128
  33.7 11.4 %collective-permute-start.11 = (bf16[4,6,48,128]{3,2,1,0:T(8,128)(2,1)S(1)}, bf16[4,6,48,128]{3,2,1,0:T(8,128)(2,1)S(1)}, u32[]{:S(2)}, u32[]{:S(2)}) collective-permute-start(bf16[4,6,48,128]{3,2,1,0:T(8,128)(2,1)S(1)} %collective-permute-done.10.refs_4_), channel_id=1, source_target_pairs={{2,3},{6,7},{10,11},{14,15},{18,19},{22,23},{26,27},{30,31},{34,35... | collective-permute-start | bytes 884744 | tf_op jit(solution)/shard_map/ppermute | solution.py:127
  86.6 8.7 %collective-permute-start.12 = (f32[96,128]{1,0:T(8,128)S(1)}, f32[96,128]{1,0:T(8,128)S(1)}, u32[]{:S(2)}, u32[]{:S(2)}) collective-permute-start(f32[96,128]{1,0:T(8,128)S(1)} %far_sum.1.mine_ref), channel_id=1, source_target_pairs={{0,32},{32,0},{1,33},{33,1},{2,34},{34,2},{3,35},{35,3},{4,36},{36... | collective-permute-start | bytes 147464 | tf_op jit(solution)/shard_map/ppermute | solution.py:189
